TPU v7x, 512 devices: a whole 4x4x16 slice. The times are simulated.
512 devices in a mesh: kt: 128 (over x, y, z_lo, core), en: 4 (over z_hi).
Axes of the slice: x: 4, y: 4, z: 16 (z_hi: 4, z_lo: 4; z = z_hi * 4 + z_lo), core: 2. Of those that a mesh axis runs over, the one named last changes fastest.
Arguments:
- counts: int32 [128], P('kt'), may hold values from 1 to 4, 256 in all
- contact_slabs: int32 [2], replicated, may hold values from 0 to 15
- onsite: float32 [16, 384], P('en'), may hold values from -0.5 to 0.5
- hopping: float32 [16, 384], P('en'), may hold values from 0.1 to 0.5
- potential_in: float32 [16, 384], P('en'), may hold values from -2 to 2
- couple_base: bfloat16 [16, 384, 384], P('en'), may hold values from -0.25 to 0.25
- couple_wave: bfloat16 [16, 384, 384], P('en'), may hold values from -0.25 to 0.25
- doping: float32 [16, 384], P('en'), may hold values from 0 to 2
- poisson_inverse: float32 [384, 384], replicated, may hold values from -0.3125 to 0.3125
Outputs:
- electron_populace: float32 [16, 384], P('en')
- potential_out: float32 [16, 384], P('en')
Inputs may be any that keep to these rules, and one draw needn't show every extreme that they name: counts sum to 256 and the largest is 4.
All inputs are finite; a program needn't handle non-finite values. No bound on the sum of `counts` on one device may be relied on, other than what follows from the above.
Results may differ from a plain program's by a relative error of at most 0.00045.
Values may be sent and summed in bfloat16 or wider, within the bound.
A program may use at most 64 MiB of HBM per device.

v0:
```python
import jax
import jax.numpy as jnp
from jax import lax
from jax.sharding import PartitionSpec as P

EMAX = 4


bottom_sample_mark = -1.0
sample_gap = 0.25
electrode_filling = -0.5
boltzmann_spread = 0.1
broadening = 1.0
contact_width = 0.5


def from_behind(block, axis, distance):
    devices = range(lax.axis_size(axis))
    route = [(i - distance, i) for i in devices if i - distance in devices]
    return lax.ppermute(block, axis, route)


def entry_amounts(transverse_impulse, eigen_height, impulse_count):
    wave_vector_number = jnp.pi * (transverse_impulse.astype(jnp.float32) + 0.5) / impulse_count
    angular_projection = jnp.cos(wave_vector_number)
    occupancy_mark = bottom_sample_mark + sample_gap * eigen_height.astype(jnp.float32)
    summation_multiplier = (
        sample_gap
        / (1.0 + jnp.exp((occupancy_mark - electrode_filling) / boltzmann_spread))
        / jnp.pi
    )
    return (angular_projection, occupancy_mark, summation_multiplier)


def slab_step(carried, couple_base, couple_wave, angular_projection, diag_real, diag_imag):
    coupled = (
        couple_base.astype(jnp.float32) + angular_projection * couple_wave.astype(jnp.float32)
    ).astype(jnp.bfloat16)
    left_part = jnp.einsum(
        "rm,pmn->prn", coupled, carried, preferred_element_type=jnp.float32
    ).astype(jnp.bfloat16)
    self_energy = jnp.einsum("prn,cn->prc", left_part, coupled, preferred_element_type=jnp.float32)
    magnitude = diag_real * diag_real + diag_imag * diag_imag
    inv_real = diag_real / magnitude
    inv_imag = -diag_imag / magnitude
    half_real = inv_real[:, None] * self_energy[0] - inv_imag[:, None] * self_energy[1]
    half_imag = inv_real[:, None] * self_energy[1] + inv_imag[:, None] * self_energy[0]
    identity = jnp.eye(diag_real.shape[0], dtype=jnp.float32)
    green_real = (
        half_real * inv_real[None, :] - half_imag * inv_imag[None, :] + identity * inv_real[None, :]
    )
    green_imag = (
        half_real * inv_imag[None, :] + half_imag * inv_real[None, :] + identity * inv_imag[None, :]
    )
    return (jnp.stack([green_real, green_imag]).astype(jnp.bfloat16), -jnp.diagonal(green_imag))


def slab_chain(carried, item_cos, item_energy, item_weight, tables):

    def one_slab(blocks, slab_row):
        couple_one, wave_one, real_row, hop_row, imag_value = slab_row
        diag_real = item_energy + real_row - item_cos * hop_row
        imag_row = jnp.full(real_row.shape, 1.0, jnp.float32) * imag_value
        blocks, diag_part = slab_step(blocks, couple_one, wave_one, item_cos, diag_real, imag_row)
        return (blocks, item_weight * diag_part)

    return lax.scan(one_slab, carried, tables)


def body(
    counts,
    contact_slabs,
    onsite,
    hopping,
    potential_in,
    couple_base,
    couple_wave,
    doping,
    poisson_inverse,
):
    kt_size = lax.axis_size("kt")
    en_size = lax.axis_size("en")
    position = lax.axis_index("en")
    mom_dev = counts.shape[0]
    impulse_count = mom_dev * kt_size
    slab_dev = onsite.shape[0]
    orbitals = onsite.shape[1]
    slot_index = jnp.arange(mom_dev * EMAX, dtype=jnp.int32)
    slot_momentum = slot_index // EMAX
    eigen_height = slot_index % EMAX
    transverse_impulse = lax.axis_index("kt") * mom_dev + slot_momentum
    selector = (jnp.arange(mom_dev, dtype=jnp.int32)[None, :] == slot_momentum[:, None]).astype(
        jnp.int32
    )
    live_count = jnp.sum(selector * counts[None, :], axis=1)
    live_mask = (eigen_height < live_count).astype(jnp.float32)
    angular_projection, occupancy_mark, summation_multiplier = entry_amounts(
        transverse_impulse, eigen_height, impulse_count
    )
    summation_multiplier = summation_multiplier * live_mask
    item_total = angular_projection.shape[0]
    real_base = -onsite - potential_in
    slab_ids = position * slab_dev + jnp.arange(slab_dev, dtype=jnp.int32)
    contact_flag = jnp.any(slab_ids[:, None] == contact_slabs[None, :], axis=1).astype(jnp.float32)
    diag_imag = broadening + contact_width * contact_flag
    tables = (couple_base, couple_wave, real_base, hopping, diag_imag)
    group_count = item_total // item_total
    section_count = group_count + en_size - 1

    def step_forward(injected_from_lead, first_item):

        def each_entry_share(values):
            carried, item_cos, item_energy, item_weight = values
            return slab_chain(carried, item_cos, item_energy, item_weight, tables)

        emitted_flux, parts = lax.map(
            each_entry_share,
            (injected_from_lead, angular_projection, occupancy_mark, summation_multiplier),
        )
        return (emitted_flux, jnp.sum(parts, axis=0))

    def stand_still(injected_from_lead, first_item):
        return (jnp.zeros_like(injected_from_lead), jnp.zeros((slab_dev, orbitals), jnp.float32))

    def section_body(section, carry):
        injected_from_lead, density_now = carry
        group_turn = section - position
        active = jnp.logical_and(group_turn >= 0, group_turn < group_count)
        first_item = jnp.clip(group_turn, 0, group_count - 1) * item_total
        emitted_flux, density_part = lax.cond(
            active, step_forward, stand_still, injected_from_lead, first_item
        )
        injected_from_lead = from_behind(emitted_flux, "en", 1)
        return (injected_from_lead, density_now + density_part)

    start_blocks = jnp.zeros((item_total, 2, orbitals, orbitals), jnp.bfloat16)
    start_density = jnp.zeros((slab_dev, orbitals), jnp.float32)
    last_blocks, electron_populace = lax.fori_loop(
        0, section_count, section_body, (start_blocks, start_density)
    )
    summed = lax.psum(electron_populace, "kt")
    potential_out = jnp.dot(summed - doping, poisson_inverse.T, precision=lax.Precision.HIGHEST)
    return (summed, potential_out)


def solution(mesh):
    return jax.shard_map(
        body,
        mesh=mesh,
        in_specs=(
            P("kt"),
            P(),
            P("en", None),
            P("en", None),
            P("en", None),
            P("en", None, None),
            P("en", None, None),
            P("en", None),
            P(),
        ),
        out_specs=(P("en", None), P("en", None)),
        check_vma=False,
    )
```

profile of v0, /device:TPU:384, one launch (start us, length us, event | category | flops | bytes accessed | tf_op | source)
XLA Modules:
  0.0 1689.7 jit_solution(8723139969726472116)
XLA Ops:
  3.9 1336.4 %while.42 = (s32[]{:T(128)}, bf16[4,2,384,384]{3,2,1,0:T(8,128)(2,1)}, f32[4,384]{1,0:T(4,128)S(1)}, s32[]{:T(128)}, f32[4,384]{1,0:T(4,128)S(1)}, /*index=5*/f3...) while((s32[]{:T(128)}, ...), condition=%wide.region_9.10_spmd.clone, body=%wide.region_1.9_spmd.clone.sunk | while | flops 459634752 | bytes 19570456 | solution.py:138
  6.9 59.7 %collective-permute-done = bf16[4,2,384,384]{3,2,1,0:T(8,128)(2,1)} collective-permute-done((bf16[4,2,384,384]{3,2,1,0:T(8,128)(2,1)}, bf16[4,2,384,384]{3,2,1,0:T(8,128)(2,1)}, u32[]{:S(2)}, u32[]{:S(2)}) %collective-permute-start) | collective-permute-done | bytes 2359328 | tf_op jit(solution)/shard_map/while/body/eval_jaxpr/ppermute | solution.py:20
  69.6 199.1 %collective-permute-done = bf16[4,2,384,384]{3,2,1,0:T(8,128)(2,1)} collective-permute-done((bf16[4,2,384,384]{3,2,1,0:T(8,128)(2,1)}, bf16[4,2,384,384]{3,2,1,0:T(8,128)(2,1)}, u32[]{:S(2)}, u32[]{:S(2)}) %collective-permute-start) | collective-permute-done | bytes 2359328 | tf_op jit(solution)/shard_map/while/body/eval_jaxpr/ppermute | solution.py:20
  271.6 513.3 %collective-permute-done = bf16[4,2,384,384]{3,2,1,0:T(8,128)(2,1)} collective-permute-done((bf16[4,2,384,384]{3,2,1,0:T(8,128)(2,1)}, bf16[4,2,384,384]{3,2,1,0:T(8,128)(2,1)}, u32[]{:S(2)}, u32[]{:S(2)}) %collective-permute-start) | collective-permute-done | bytes 2359328 | tf_op jit(solution)/shard_map/while/body/eval_jaxpr/ppermute | solution.py:20
  784.9 211.7 %conditional.3 = (bf16[4,2,384,384]{3,2,1,0:T(8,128)(2,1)}, f32[4,384]{1,0:T(4,128)S(1)}) conditional(s32[]{:T(128)} %convert_element_type.89, () %tuple.154, (bf16[4,2,384,384]{3,2,1,0:T(8,128)(2,1)}, f32[4]{0:T(128)S(1)}, f32[4]{0:T(128)S(1)}, s32[4]{0:T(128)S(1)}, f32[4,384]{1,0:T(4,128)S(1)}, /*index=5*/f32[4,384]{1,0:T(4,128)}, ...), branch_computations={%region_2.2_spmd, %region_3.8_spmd.clone} | conditional | flops 459631552 | bytes 10114378 | solution.py:130
  785.7 210.9 %while.41 = (s32[]{:T(128)}, bf16[4,2,384,384]{3,2,1,0:T(8,128)(2,1)}, f32[4,4,384]{2,1,0:T(4,128)S(1)}, bf16[4,2,384,384]{3,2,1,0:T(8,128)(2,1)}, f32[4]{0:T(12...) while((s32[]{:T(128)}, ...), condition=%wide.region_7.6_spmd, body=%wide.region_4.5_spmd.sunk | while | flops 459626880 | bytes 10083334 | solution.py:116
  788.7 48.8 %while.43 = (s32[]{:T(128)}, bf16[2,384,384]{2,1,0:T(8,128)(2,1)S(1)}, f32[4,384]{1,0:T(4,128)S(1)}, f32[]{:T(128)}, f32[4,384]{1,0:T(4,128)S(1)}, /*index=5*/f3...) while((s32[]{:T(128)}, ...), condition=%wide.region_6.4_spmd, body=%wide.region_5.3_spmd.sunk | while | flops 459626880 | bytes 7711433 | solution.py:67
  793.4 2.6 fusion.47
  796.7 3.4 gather_fusion
  805.6 2.6 fusion.47
  808.9 3.4 gather_fusion
  817.8 2.6 fusion.47
  821.1 3.4 gather_fusion
  828.1 2.0 fusion.46
  830.0 2.6 fusion.47
  833.3 3.4 gather_fusion
  841.4 48.8 %while.43 = (s32[]{:T(128)}, bf16[2,384,384]{2,1,0:T(8,128)(2,1)S(1)}, f32[4,384]{1,0:T(4,128)S(1)}, f32[]{:T(128)}, f32[4,384]{1,0:T(4,128)S(1)}, /*index=5*/f3...) while((s32[]{:T(128)}, ...), condition=%wide.region_6.4_spmd, body=%wide.region_5.3_spmd.sunk | while | flops 459626880 | bytes 7711433 | solution.py:67
  844.2 2.0 fusion.46
  846.1 2.6 fusion.47
  849.4 3.4 gather_fusion
  858.3 2.6 fusion.47
  861.6 3.4 gather_fusion
  870.5 2.6 fusion.47
  873.8 3.4 gather_fusion
  882.8 2.6 fusion.47
  886.0 3.4 gather_fusion
  894.1 48.8 %while.43 = (s32[]{:T(128)}, bf16[2,384,384]{2,1,0:T(8,128)(2,1)S(1)}, f32[4,384]{1,0:T(4,128)S(1)}, f32[]{:T(128)}, f32[4,384]{1,0:T(4,128)S(1)}, /*index=5*/f3...) while((s32[]{:T(128)}, ...), condition=%wide.region_6.4_spmd, body=%wide.region_5.3_spmd.sunk | while | flops 459626880 | bytes 7711433 | solution.py:67
  896.9 2.0 fusion.46
  898.8 2.6 fusion.47
  902.1 3.4 gather_fusion
  909.1 2.0 fusion.46
  911.1 2.6 fusion.47
  914.3 3.4 gather_fusion
  923.3 2.6 fusion.47
  926.5 3.4 gather_fusion
  935.5 2.6 fusion.47
  938.7 3.4 gather_fusion
  946.9 48.8 %while.43 = (s32[]{:T(128)}, bf16[2,384,384]{2,1,0:T(8,128)(2,1)S(1)}, f32[4,384]{1,0:T(4,128)S(1)}, f32[]{:T(128)}, f32[4,384]{1,0:T(4,128)S(1)}, /*index=5*/f3...) while((s32[]{:T(128)}, ...), condition=%wide.region_6.4_spmd, body=%wide.region_5.3_spmd.sunk | while | flops 459626880 | bytes 7711433 | solution.py:67
  951.6 2.6 fusion.47
  954.8 3.4 gather_fusion
  963.8 2.6 fusion.47
  967.0 3.4 gather_fusion
  976.0 2.6 fusion.47
  979.3 3.4 gather_fusion
  988.2 2.6 fusion.47
  991.5 3.4 gather_fusion
  997.9 342.4 %collective-permute-done = bf16[4,2,384,384]{3,2,1,0:T(8,128)(2,1)} collective-permute-done((bf16[4,2,384,384]{3,2,1,0:T(8,128)(2,1)}, bf16[4,2,384,384]{3,2,1,0:T(8,128)(2,1)}, u32[]{:S(2)}, u32[]{:S(2)}) %collective-permute-start) | collective-permute-done | bytes 2359328 | tf_op jit(solution)/shard_map/while/body/eval_jaxpr/ppermute | solution.py:20
  1340.3 348.0 %psum.7 = f32[4,384]{1,0:T(4,128)S(1)} all-reduce(f32[4,384]{1,0:T(4,128)S(1)} %get-tuple-element.351), channel_id=1, replica_groups=mesh['kt'=128,'en'=4] {'kt'}, use_global_device_ids=true, to_apply=%region_10.11 | all-reduce | flops 1536 | bytes 12288 | tf_op jit(solution)/shard_map/psum | solution.py:141
  (239 shorter events, 92.3 us)
Async XLA Ops:
  0.6 1687.8 %copy-start = (f32[384,384]{1,0:T(8,128)S(1)}, f32[384,384]{1,0:T(8,128)}, u32[]{:S(2)}) copy-start(f32[384,384]{1,0:T(8,128)} %param.25) | copy-start | bytes 1769476
  3.9 1684.5 %copy-start.2 = (f32[4,384]{1,0:T(4,128)S(1)}, f32[4,384]{1,0:T(4,128)}, u32[]{:S(2)}) copy-start(f32[4,384]{1,0:T(4,128)} %param.24) | copy-start | bytes 18436
  5.6 61.0 %collective-permute-start = (bf16[4,2,384,384]{3,2,1,0:T(8,128)(2,1)}, bf16[4,2,384,384]{3,2,1,0:T(8,128)(2,1)}, u32[]{:S(2)}, u32[]{:S(2)}) collective-permute-start(bf16[4,2,384,384]{3,2,1,0:T(8,128)(2,1)} %get-tuple-element.768), channel_id=1, source_target_pairs={{0,1},{1,2},{2,3},{4,5},{5,6},{6,7},{8,9},{9,10},{10,11},{12,13},{... | collective-permute-start | bytes 7077896 | tf_op jit(solution)/shard_map/while/body/eval_jaxpr/ppermute | solution.py:20
  68.2 200.4 %collective-permute-start = (bf16[4,2,384,384]{3,2,1,0:T(8,128)(2,1)}, bf16[4,2,384,384]{3,2,1,0:T(8,128)(2,1)}, u32[]{:S(2)}, u32[]{:S(2)}) collective-permute-start(bf16[4,2,384,384]{3,2,1,0:T(8,128)(2,1)} %get-tuple-element.768), channel_id=1, source_target_pairs={{0,1},{1,2},{2,3},{4,5},{5,6},{6,7},{8,9},{9,10},{10,11},{12,13},{... | collective-permute-start | bytes 7077896 | tf_op jit(solution)/shard_map/while/body/eval_jaxpr/ppermute | solution.py:20
  270.3 514.6 %collective-permute-start = (bf16[4,2,384,384]{3,2,1,0:T(8,128)(2,1)}, bf16[4,2,384,384]{3,2,1,0:T(8,128)(2,1)}, u32[]{:S(2)}, u32[]{:S(2)}) collective-permute-start(bf16[4,2,384,384]{3,2,1,0:T(8,128)(2,1)} %get-tuple-element.768), channel_id=1, source_target_pairs={{0,1},{1,2},{2,3},{4,5},{5,6},{6,7},{8,9},{9,10},{10,11},{12,13},{... | collective-permute-start | bytes 7077896 | tf_op jit(solution)/shard_map/while/body/eval_jaxpr/ppermute | solution.py:20
  996.6 343.7 %collective-permute-start = (bf16[4,2,384,384]{3,2,1,0:T(8,128)(2,1)}, bf16[4,2,384,384]{3,2,1,0:T(8,128)(2,1)}, u32[]{:S(2)}, u32[]{:S(2)}) collective-permute-start(bf16[4,2,384,384]{3,2,1,0:T(8,128)(2,1)} %get-tuple-element.768), channel_id=1, source_target_pairs={{0,1},{1,2},{2,3},{4,5},{5,6},{6,7},{8,9},{9,10},{10,11},{12,13},{... | collective-permute-start | bytes 7077896 | tf_op jit(solution)/shard_map/while/body/eval_jaxpr/ppermute | solution.py:20
  1688.4 1.2 copy-start.1
where the time goes:
time: 1690 us
  waiting for transfers between devices  1110 us (66%)
  blocking collectives  348 us (21%)
  local copies, waits for them, and re-layouts  88.4 us (5%)
  other arithmetic  55.6 us (3%)
  matrix products  43.2 us (3%)
  loops' own time  34.1 us (2%)
    ppermute x4, waiting for transfers between devices, from_behind(): return lax.ppermute(block, axis, route)  1110 us
    psum x1, blocking collectives, body(): summed = lax.psum(electron_populace, 'kt')  348 us
    gather x16, local copies, waits for them, and re-layouts, slab_step(): jnp.diagonal(green_imag)  55.1 us
    dot_general x16, matrix products, slab_step(): jnp.einsum('prn,cn->prc', left_part, coupled, preferred_element_type=jnp....  41.9 us
    another operation x4, loops' own time, slab_chain(): return lax.scan(one_slab, carried, tables)  33.8 us
  transfers between devices with their start and end apart: 4, of which 4 were waited for; matrix products, arithmetic and copies ran while one was open for 0% of the time, Pallas kernels for 0%

commit v1 on v0

v1 whole, which is shorter than its diff:
```python
import functools
import jax, jax.numpy as jnp
from jax import lax
from jax.experimental import pallas as pl
from jax.experimental.pallas import tpu as pltpu
from jax.sharding import PartitionSpec as P

NT = (((1,), (1,)), ((), ()))
f32, bf16 = jnp.float32, jnp.bfloat16

def chain_kernel(sym, scal_ref, tab_ref, w_ref, out_ref, g_ref, l_ref, c_ref):
    s = pl.program_id(0)
    n = w_ref.shape[-1]
    nb = n // 128
    cos, energy, weight = scal_ref[0], scal_ref[1], scal_ref[2]
    row = tab_ref[0]
    dr = energy + row[0:1] - cos * row[1:2]
    di = row[2:3]
    mag = dr * dr + di * di
    br = dr / mag
    bi = -di / mag
    eye = lax.broadcasted_iota(jnp.int32, (128, 128), 0) == lax.broadcasted_iota(jnp.int32, (128, 128), 1)
    brc = jnp.transpose(jnp.broadcast_to(br, (128, n)))
    bic = jnp.transpose(jnp.broadcast_to(bi, (128, n)))

    @pl.when(s == 0)
    def _():
        g_ref[...] = jnp.zeros_like(g_ref)
        for i in range(nb):
            sl = slice(128 * i, 128 * i + 128)
            g_ref[256 * i:256 * i + 128, sl] = jnp.where(eye, br[:, sl], 0.0).astype(bf16)
            g_ref[256 * i + 128:256 * i + 256, sl] = jnp.where(eye, bi[:, sl], 0.0).astype(bf16)
        out_ref[0] = -weight * bi

    @pl.when(s > 0)
    def _():
        c_ref[...] = (w_ref[0].astype(f32) + cos * w_ref[1].astype(f32)).astype(bf16)
        c = c_ref[...]
        for j in range(nb):
            L = lax.dot_general(c, g_ref[256 * j:256 * j + 256, :], NT, preferred_element_type=f32).astype(bf16)
            for i in range(nb):
                l_ref[256 * i:256 * i + 128, 128 * j:128 * j + 128] = L[128 * i:128 * i + 128, 0:128]
                l_ref[256 * i + 128:256 * i + 256, 128 * j:128 * j + 128] = L[128 * i:128 * i + 128, 128:256]
        for j in range(nb):
            lo = 128 * j if sym else 0
            sl = slice(128 * j, 128 * j + 128)
            SE = lax.dot_general(c_ref[lo:, :], l_ref[256 * j:256 * j + 256, :], NT, preferred_element_type=f32)
            for i in range(lo // 128, nb):
                se_r, se_i = SE[128 * i - lo:128 * i - lo + 128, :128], SE[128 * i - lo:128 * i - lo + 128, 128:]
                cr, ci = brc[128 * i:128 * i + 128], bic[128 * i:128 * i + 128]
                hr = cr * se_r - ci * se_i
                hi = cr * se_i + ci * se_r
                rr, ri = br[:, sl], bi[:, sl]
                gr = hr * rr - hi * ri
                gi = hr * ri + hi * rr
                if i == j:
                    gr = gr + jnp.where(eye, rr, 0.0)
                    gi = gi + jnp.where(eye, ri, 0.0)
                    out_ref[0, :, sl] = -weight * jnp.sum(jnp.where(eye, gi, 0.0), axis=0, keepdims=True)
                gr, gi = gr.astype(bf16), gi.astype(bf16)
                g_ref[256 * i:256 * i + 128, sl] = gr
                g_ref[256 * i + 128:256 * i + 256, sl] = gi
                if sym and i > j:
                    si = slice(128 * i, 128 * i + 128)
                    g_ref[256 * j:256 * j + 128, si] = jnp.transpose(gr)
                    g_ref[256 * j + 128:256 * j + 256, si] = jnp.transpose(gi)

def chain(scal, tab, w, sym=False):
    S, n = w.shape[0], w.shape[-1]
    return pl.pallas_call(
        functools.partial(chain_kernel, sym),
        grid=(S,),
        in_specs=[
            pl.BlockSpec(memory_space=pltpu.SMEM),
            pl.BlockSpec((1, 3, n), lambda s: (s, 0, 0)),
            pl.BlockSpec((None, 2, n, n), lambda s: (s, 0, 0, 0)),
        ],
        out_specs=pl.BlockSpec((1, 1, n), lambda s: (s, 0, 0)),
        out_shape=jax.ShapeDtypeStruct((S, 1, n), f32),
        scratch_shapes=[pltpu.VMEM((2 * n, n), bf16), pltpu.VMEM((2 * n, n), bf16), pltpu.VMEM((n, n), bf16)],
        compiler_params=pltpu.CompilerParams(vmem_limit_bytes=48 * 2**20),
    )(scal, tab, w)


ENERGIES = 4
BOTTOM, GAP, FILLING, SPREAD = -1.0, 0.25, -0.5, 0.1
BROADENING, CONTACT = 1.0, 0.5


def body(counts, contact_slabs, onsite, hopping, potential_in, couple_base, couple_wave, doping, poisson_inverse):
    kt_size, en_size = lax.axis_size("kt"), lax.axis_size("en")
    q, e = lax.axis_index("kt"), lax.axis_index("en")
    slabs, n = onsite.shape
    cos = jnp.cos(jnp.pi * (q.astype(f32) + 0.5) / kt_size)
    energy = BOTTOM + GAP * e.astype(f32)
    weight = GAP / (1.0 + jnp.exp((energy - FILLING) / SPREAD)) / jnp.pi
    weight = jnp.where(e < counts[0], weight, 0.0)
    slab_ids = e * slabs + jnp.arange(slabs, dtype=jnp.int32)
    contact = jnp.any(slab_ids[:, None] == contact_slabs[None, :], axis=1).astype(f32)
    imag = jnp.broadcast_to((BROADENING + CONTACT * contact)[:, None], (slabs, n))
    tab = lax.all_gather(jnp.stack([-onsite - potential_in, hopping, imag], 1), "en", tiled=True)
    rows = slabs * 2 * n // kt_size
    per = n // rows
    which = lax.rem(q // per, 2)
    place = (q // (2 * per), lax.rem(q, per) * rows, 0)
    piece = jnp.where(which == 0, lax.dynamic_slice(couple_base, place, (1, rows, n)),
                      lax.dynamic_slice(couple_wave, place, (1, rows, n)))[0]
    w = lax.all_gather(piece, ("kt", "en"), tiled=True).reshape(slabs, 2 * per, en_size, rows, n)
    w = w.transpose(2, 0, 1, 3, 4).reshape(slabs * en_size, 2, n, n)
    density = chain(jnp.stack([cos, energy, weight]), tab, w, True)[:, 0]
    density = lax.psum_scatter(density, "en", scatter_dimension=0, tiled=True)
    summed = lax.psum(density, "kt")
    potential_out = jnp.dot(summed - doping, poisson_inverse.T, precision=lax.Precision.HIGHEST)
    return summed, potential_out


def solution(mesh):
    return jax.shard_map(
        body,
        mesh=mesh,
        in_specs=(P("kt"), P(), P("en", None), P("en", None), P("en", None), P("en", None, None), P("en", None, None),
                  P("en", None), P()),
        out_specs=(P("en", None), P("en", None)),
        check_vma=False,
    )
```

time: 1690 us -> 1840 us (1.089)
  the two profiles are of different devices: /device:TPU:384 before, /device:TPU:1 now
where the time goes in v1:
time: 1840 us
  waiting for transfers between devices  1400 us (76%)
  blocking collectives  390 us (21%)
  Pallas kernels  18.7 us (1%)
    all_gather x1, waiting for transfers between devices, body(): lax.all_gather(piece, ('kt', 'en'), tiled=True)  1400 us
    psum x1, blocking collectives, body(): summed = lax.psum(density, 'kt')  338 us
  transfers between devices with their start and end apart: 1, of which 1 were waited for; matrix products, arithmetic and copies ran while one was open for 0% of the time, Pallas kernels for 0%

profile of v1, /device:TPU:1, one launch (start us, length us, event | category | flops | bytes accessed | tf_op | source)
XLA Modules:
  0.0 1836.5 jit_solution(4362299992848021594)
XLA Ops:
  7.2 0.0 copy-start
  7.2 0.0 all-gather.3.cloned.1.call-start
  7.3 1.4 dynamic-slice_select_fusion
  8.7 0.0 all-gather.3.cloned.1.call-update
  9.5 0.7 negate_subtract_fusion
  10.3 0.7 stack.26
  11.0 1.3 dynamic-slice
  12.9 0.8 compare_reduce_fusion
  13.7 0.1 stack_broadcast_in_dim.2
  13.8 23.8 %all_gather.6.tab_ref = f32[16,3,384]{2,1,0:T(4,128)S(1)} all-gather(f32[4,3,384]{2,1,0:T(4,128)S(1)} %pad_maximum_fusion), channel_id=1, replica_groups=mesh['kt'=128,'en'=4] {'en'}, dimensions={0}, use_global_device_ids=true | all-gather | bytes 92160 | tf_op jit(solution)/shard_map/all_gather | solution.py:101
  37.6 0.1 pad_maximum_fusion.1.scal_ref
  37.7 1397.2 %all-gather.3.cloned.1.call-done = bf16[1,12288,384]{2,1,0:T(8,128)(2,1)} async-done(((bf16[1,24,384]{2,1,0:T(8,128)(2,1)}), bf16[1,12288,384]{2,1,0:T(8,128)(2,1)}) %all-gather.3.cloned.1.call-update) | async-done | bytes 9437200 | tf_op jit(solution)/shard_map/all_gather | solution.py:108
  1434.9 9.0 copy.13
  1443.9 0.0 copy-start.2
  1443.9 18.7 %shard_map.104 = f32[16,1,384]{2,1,0:T(1,128)S(1)} custom-call(f32[3]{0:T(128)S(1)} %pad_maximum_fusion.1.scal_ref, f32[16,3,384]{2,1,0:T(4,128)S(1)} %all_gather.6.tab_ref, bf16[16,2,384,384]{3,2,1,0:T(8,128)(2,1)} %bitcast.14), custom_call_target="tpu_custom_call" | custom-call | tf_op jit(solution)/shard_map/pallas_call | solution.py:70
  1462.6 28.0 %all-reduce = f32[16,384]{1,0:T(8,128)S(1)} all-reduce(f32[16,384]{1,0:T(8,128)S(1)} %bitcast.16), channel_id=3, replica_groups=mesh['kt'=128,'en'=4] {'en'}, use_global_device_ids=true, to_apply=%region_1.2.clone | all-reduce | flops 6144 | bytes 49152
  1490.6 337.7 %psum.7 = f32[4,384]{1,0:T(4,128)S(1)} all-reduce(f32[4,384]{1,0:T(4,128)S(1)} %constant_dynamic-slice_fusion), channel_id=1, replica_groups=mesh['kt'=128,'en'=4] {'kt'}, use_global_device_ids=true, to_apply=%region_2.3 | all-reduce | flops 1536 | bytes 12288 | tf_op jit(solution)/shard_map/psum | solution.py:112
  1828.4 0.0 copy-done
  1828.4 0.0 copy-done.2
  1828.4 0.0 copy-start.1
  1828.4 1.2 fusion
  1829.6 0.0 copy-done.1
  (6 shorter events, 0.1 us)
Async XLA Ops:
  7.2 1821.2 %copy-start = (f32[384,384]{1,0:T(8,128)S(1)}, f32[384,384]{1,0:T(8,128)}, u32[]{:S(2)}) copy-start(f32[384,384]{1,0:T(8,128)} %param.17) | copy-start | bytes 1769476
  7.2 1427.7 %all-gather.3.cloned.1.call-start = ((), (), s32[]{:S(2)}) async-start(), calls=%async_computation | async-start | bytes 9455616 | tf_op jit(solution)/shard_map/all_gather | solution.py:108
  1443.9 384.5 %copy-start.2 = (f32[4,384]{1,0:T(4,128)S(1)}, f32[4,384]{1,0:T(4,128)}, u32[]{:S(2)}) copy-start(f32[4,384]{1,0:T(4,128)} %param.16) | copy-start | bytes 18436
  1828.4 1.2 copy-start.1
Sparse Core Ops, SparseCore 0:
  10.3 1424.6 all-gather.2

commit v2 on v1

v2 whole, which is shorter than its diff:
```python
import jax
import jax.numpy as jnp
from jax import lax
from jax.experimental import pallas as pl
from jax.experimental.pallas import tpu as pltpu
from jax.sharding import PartitionSpec as P

f32, bf16 = jnp.float32, jnp.bfloat16
NT = (((1,), (1,)), ((), ()))
MESH = pl.DeviceIdType.MESH

BOTTOM, GAP, FILLING, SPREAD = -1.0, 0.25, -0.5, 0.1
BROADENING, CONTACT = 1.0, 0.5
NX, NY, NZ, EN, CORES = 4, 4, 4, 4, 2
LANES = 128
AHEAD_ROW, AHEAD_PLANE, AHEAD_CHIP = 5, 3, 1


def kernel(
    scal_ref, contact_ref, tab_in, base_ref, wave_ref, doping_ref, inverse_ref,
    den_out, pot_out,
    w_ref, tab_ref, g_ref, l_ref, c_ref, den_ref, sib_ref, chip_ref, line_in, line_ref, plane_in,
    load_sem, tab_sems, z_sems, row_sems, plane_sems, chip_sems, sib_sems, line_sems, last_sems,
):
    kt, e = lax.axis_index("kt"), lax.axis_index("en")
    x, y, zl, c = kt // 32, (kt // 8) % 4, (kt // 2) % 4, kt % 2
    z = e * NZ + zl
    slabs, n = base_ref.shape[0], base_ref.shape[-1]
    pairs = slabs * EN // CORES
    own_pairs = slabs // CORES
    blocks = n // LANES
    part = 2 * n // (NX * NY)

    def device(x, y, z, c):
        return (((x % NX) * NY + y % NY) * NZ + z % NZ) * CORES + c, (z // NZ) % EN

    def remote(src, dst, sems, index, where):
        return pltpu.make_async_remote_copy(
            src, dst, sems.at[(0, *index)], sems.at[(1, *index)], device_id=where, device_id_type=MESH
        )

    a, b = x + c * (y - x), y + c * (x - y)
    sibling = device(x, y, z, 1 - c)

    def step_row(d):
        return device(x + (1 - c) * d, y + c * d, z, c)

    def step_plane(d):
        return device(x + c * d, y + (1 - c) * d, z, c)

    def rows(first, count):
        return pl.ds(pl.multiple_of(first, 16), count)

    barrier = pltpu.get_barrier_semaphore()
    for d in range(1, NZ * EN):
        pl.semaphore_signal(barrier, 1, device_id=device(x, y, (z + d) % (NZ * EN), c), device_id_type=MESH)
    for d in range(1, NX * NY):
        pl.semaphore_signal(barrier, 1, device_id=device(x + d // NY, y + d % NY, z, c), device_id_type=MESH)
    pl.semaphore_signal(barrier, 1, device_id=sibling, device_id_type=MESH)

    def loads(i):
        s = e * slabs + i
        return (
            pltpu.make_async_copy(base_ref.at[i], w_ref.at[s, :n], load_sem.at[0, i]),
            pltpu.make_async_copy(wave_ref.at[i], w_ref.at[s, n:], load_sem.at[1, i]),
        )

    for i in range(slabs):
        for copy in loads(i):
            copy.start()
    tab_ref[e] = tab_in[...]
    pl.semaphore_wait(barrier, NZ * EN + NX * NY - 1)

    def send_tab(d):
        return remote(tab_in, tab_ref.at[e], tab_sems, (d - 1,), (kt, (e + d) % EN))

    def send_z(i, d):
        k = e * own_pairs + i
        piece = rows(part * (4 * b + a), part)
        here = w_ref.at[2 * k + c, piece]
        return remote(here, here, z_sems, (i, d - 1), (kt, (e + d) % EN))

    def wait_z(k):
        piece = w_ref.at[2 * k + c, rows(part * (4 * b + a), part)]
        d = (e - k // own_pairs + EN) % EN
        remote(piece, piece, z_sems, (k % own_pairs, d - 1), sibling).wait_recv()

    def send_row(k, d):
        here = w_ref.at[2 * k + c, rows(part * (4 * b + a), part)]
        return remote(here, here, row_sems, (k, d - 1), step_row(d))

    def send_plane(k, d):
        here = w_ref.at[2 * k + c, rows(part * 4 * b, 4 * part)]
        return remote(here, here, plane_sems, (k, d - 1), step_plane(d))

    def send_chip(k):
        here = w_ref.at[2 * k + c]
        return remote(here, here, chip_sems, (k,), sibling)

    def foreign(k):
        return jnp.logical_and(jnp.logical_and(k >= 0, k < pairs), k // own_pairs != e)

    def advance(k):
        at_row, at_plane, at_chip = k + AHEAD_ROW, k + AHEAD_PLANE, k + AHEAD_CHIP

        @pl.when(foreign(at_row))
        def _():
            wait_z(at_row)
            for d in range(1, 4):
                send_row(at_row, d).start()

        @pl.when(foreign(at_plane))
        def _():
            for d in range(1, 4):
                send_row(at_plane, d).wait_recv()
            for d in range(1, 4):
                send_plane(at_plane, d).start()

        @pl.when(foreign(at_chip))
        def _():
            for d in range(1, 4):
                send_plane(at_chip, d).wait_recv()
            send_chip(at_chip).start()

    for d in range(1, EN):
        send_tab(d).start()
    for i in range(slabs):
        for copy in loads(i):
            copy.wait()
    for i in range(own_pairs):
        for d in range(1, EN):
            send_z(i, d).start()

    def prologue(k, carry):
        advance(k)
        return carry

    lax.fori_loop(-AHEAD_ROW, 0, prologue, 0)
    for d in range(1, EN):
        send_tab(d).wait_recv()

    cos, energy, weight = scal_ref[0], scal_ref[1], scal_ref[2]
    eye = lax.broadcasted_iota(jnp.int32, (LANES, LANES), 0) == lax.broadcasted_iota(jnp.int32, (LANES, LANES), 1)

    def inverse_diag(s):
        group, local = s // slabs, s % slabs
        touches = jnp.logical_or(contact_ref[0] == s, contact_ref[1] == s)
        di = BROADENING + CONTACT * touches.astype(f32)
        dr = energy + tab_ref[group, pl.ds(local, 1), :] - cos * tab_ref[group, pl.ds(slabs + local, 1), :]
        mag = dr * dr + di * di
        return dr / mag, -di / mag

    def put_density(s, j, value):
        den_ref[s // slabs, pl.ds(slabs * j + s % slabs, 1), :] = value

    den_ref[...] = jnp.zeros_like(den_ref)
    g_ref[...] = jnp.zeros_like(g_ref)
    br, bi = inverse_diag(0)
    for i in range(blocks):
        sl = slice(LANES * i, LANES * (i + 1))
        g_ref[2 * LANES * i:2 * LANES * i + LANES, sl] = jnp.where(eye, br[:, sl], 0.0).astype(bf16)
        g_ref[2 * LANES * i + LANES:2 * LANES * (i + 1), sl] = jnp.where(eye, bi[:, sl], 0.0).astype(bf16)
        put_density(0, i, -weight * bi[:, sl])

    def slab(s):
        br, bi = inverse_diag(s)
        brc = jnp.transpose(jnp.broadcast_to(br, (LANES, n)))
        bic = jnp.transpose(jnp.broadcast_to(bi, (LANES, n)))
        c_ref[...] = (w_ref[s, :n].astype(f32) + cos * w_ref[s, n:].astype(f32)).astype(bf16)
        for j in range(blocks):
            left = lax.dot_general(
                c_ref[...], g_ref[2 * LANES * j:2 * LANES * (j + 1), :], NT, preferred_element_type=f32
            ).astype(bf16)
            sl = slice(LANES * j, LANES * (j + 1))
            for i in range(blocks):
                piece = left[LANES * i:LANES * (i + 1)]
                l_ref[2 * LANES * i:2 * LANES * i + LANES, sl] = piece[:, :LANES]
                l_ref[2 * LANES * i + LANES:2 * LANES * (i + 1), sl] = piece[:, LANES:]
        for j in range(blocks):
            lo = LANES * j
            sl = slice(lo, lo + LANES)
            energy_part = lax.dot_general(
                c_ref[lo:, :], l_ref[2 * lo:2 * lo + 2 * LANES, :], NT, preferred_element_type=f32
            )
            for i in range(j, blocks):
                piece = energy_part[LANES * i - lo:LANES * (i + 1) - lo]
                se_r, se_i = piece[:, :LANES], piece[:, LANES:]
                cr, ci = brc[LANES * i:LANES * (i + 1)], bic[LANES * i:LANES * (i + 1)]
                rr, ri = br[:, sl], bi[:, sl]
                hr = cr * se_r - ci * se_i
                hi = cr * se_i + ci * se_r
                gr = hr * rr - hi * ri
                gi = hr * ri + hi * rr
                if i == j:
                    gr = gr + jnp.where(eye, rr, 0.0)
                    gi = gi + jnp.where(eye, ri, 0.0)
                    put_density(s, j, -weight * jnp.sum(jnp.where(eye, gi, 0.0), axis=0, keepdims=True))
                gr, gi = gr.astype(bf16), gi.astype(bf16)
                g_ref[2 * LANES * i:2 * LANES * i + LANES, sl] = gr
                g_ref[2 * LANES * i + LANES:2 * LANES * (i + 1), sl] = gi
                if i > j:
                    si = slice(LANES * i, LANES * (i + 1))
                    g_ref[2 * lo:2 * lo + LANES, si] = jnp.transpose(gr)
                    g_ref[2 * lo + LANES:2 * lo + 2 * LANES, si] = jnp.transpose(gi)

    def chain(s, carry):
        k = s // CORES

        @pl.when(s % CORES == 0)
        def _():
            advance(k)

            @pl.when(foreign(k))
            def _():
                there = w_ref.at[2 * k + 1 - c]
                remote(there, there, chip_sems, (k,), sibling).wait_recv()

        @pl.when(s > 0)
        def _():
            slab(s)

        return carry

    lax.fori_loop(0, slabs * EN, chain, 0)

    both = remote(den_ref, sib_ref, sib_sems, (), sibling)
    both.start()
    both.wait_recv()
    chip_ref[...] = den_ref[...] + sib_ref[...]

    def send_line(d):
        to = (z + d) % (NZ * EN)
        return remote(chip_ref.at[to // NZ], line_in.at[z], line_sems, (d - 1,), device(x, y, to, c))

    for d in range(1, NZ * EN):
        send_line(d).start()
    line_in[z] = chip_ref[e]
    for d in range(1, NZ * EN):
        remote(chip_ref.at[e], line_in.at[(z + NZ * EN - d) % (NZ * EN)], line_sems, (d - 1,), sibling).wait_recv()
    line = line_in[0]
    for i in range(1, NZ * EN):
        line = line + line_in[i]
    line_ref[...] = line

    def send_last(d):
        return remote(
            line_ref, plane_in.at[x * NY + y], last_sems, (d - 1,), device(x + d // NY, y + d % NY, z, c)
        )

    for d in range(1, NX * NY):
        send_last(d).start()
    plane_in[x * NY + y] = line
    for d in range(1, NX * NY):
        sender = ((x - d // NY + NX) % NX) * NY + (y - d % NY + NY) % NY
        remote(line_ref, plane_in.at[sender], last_sems, (d - 1,), sibling).wait_recv()
    total = plane_in[0]
    for i in range(1, NX * NY):
        total = total + plane_in[i]
    pot = jnp.zeros((slabs, n), f32)
    for j in range(blocks):
        sl = slice(LANES * j, LANES * (j + 1))
        block = total[slabs * j:slabs * (j + 1), :]
        den_out[:, sl] = block
        pot = pot + lax.dot_general(
            block - doping_ref[:, sl], inverse_ref[:, sl], NT,
            precision=lax.Precision.HIGHEST, preferred_element_type=f32,
        )
    pot_out[...] = pot

    for d in range(1, EN):
        send_tab(d).wait_send()
        for i in range(own_pairs):
            send_z(i, d).wait_send()

    def left(k, carry):
        @pl.when(foreign(k))
        def _():
            for d in range(1, 4):
                send_row(k, d).wait_send()
                send_plane(k, d).wait_send()
            send_chip(k).wait_send()

        return carry

    lax.fori_loop(0, pairs, left, 0)
    both.wait_send()
    for d in range(1, NZ * EN):
        send_line(d).wait_send()
    for d in range(1, NX * NY):
        send_last(d).wait_send()


def body(counts, contact_slabs, onsite, hopping, potential_in, couple_base, couple_wave, doping, poisson_inverse):
    kt_size = lax.axis_size("kt")
    q, e = lax.axis_index("kt"), lax.axis_index("en")
    slabs, n = onsite.shape
    cos = jnp.cos(jnp.pi * (q.astype(f32) + 0.5) / kt_size)
    energy = BOTTOM + GAP * e.astype(f32)
    weight = GAP / (1.0 + jnp.exp((energy - FILLING) / SPREAD)) / jnp.pi
    weight = jnp.where(e < counts[0], weight, 0.0)
    tab = jnp.concatenate([-onsite - potential_in, hopping], 0)
    total = slabs * EN
    pairs = total // CORES
    vmem, smem = pl.BlockSpec(memory_space=pltpu.VMEM), pl.BlockSpec(memory_space=pltpu.SMEM)
    anywhere = pl.BlockSpec(memory_space=pl.ANY)
    piece = (4 * slabs, LANES)
    sems = pltpu.SemaphoreType.DMA
    return pl.pallas_call(
        kernel,
        out_shape=(jax.ShapeDtypeStruct((slabs, n), f32), jax.ShapeDtypeStruct((slabs, n), f32)),
        in_specs=[smem, smem, vmem, anywhere, anywhere, vmem, vmem],
        out_specs=(vmem, vmem),
        scratch_shapes=[
            pltpu.VMEM((total, 2 * n, n), bf16),
            pltpu.VMEM((EN, 2 * slabs, n), f32),
            pltpu.VMEM((2 * n, n), bf16),
            pltpu.VMEM((2 * n, n), bf16),
            pltpu.VMEM((n, n), bf16),
            pltpu.VMEM((EN, *piece), f32),
            pltpu.VMEM((EN, *piece), f32),
            pltpu.VMEM((EN, *piece), f32),
            pltpu.VMEM((NZ * EN, *piece), f32),
            pltpu.VMEM(piece, f32),
            pltpu.VMEM((NX * NY, *piece), f32),
            sems((2, slabs)),
            sems((2, EN - 1)),
            sems((2, slabs // CORES, EN - 1)),
            sems((2, pairs, 3)),
            sems((2, pairs, 3)),
            sems((2, pairs)),
            sems((2,)),
            sems((2, NZ * EN - 1)),
            sems((2, NX * NY - 1)),
        ],
        compiler_params=pltpu.CompilerParams(collective_id=0, has_side_effects=True, vmem_limit_bytes=40 * 2**20),
    )(jnp.stack([cos, energy, weight]), contact_slabs, tab, couple_base, couple_wave, doping, poisson_inverse)


def solution(mesh):
    return jax.shard_map(
        body,
        mesh=mesh,
        in_specs=(
            P("kt"), P(), P("en", None), P("en", None), P("en", None),
            P("en", None, None), P("en", None, None), P("en", None), P(),
        ),
        out_specs=(P("en", None), P("en", None)),
        check_vma=False,
    )
```

time: 1840 us -> 100 us (0.05)
  waiting for transfers between devices: 1400 us -> 0 us
  blocking collectives: 390 us -> 0 us
  Pallas kernels: 18.7 us -> 90.5 us
    all_gather x1 -> x0, waiting for transfers between devices: 1400 us -> none  [body(): lax.all_gather(piece, ('kt', 'en'), tiled=True)]
    psum x1 -> x0, blocking collectives: 338 us -> none  [body(): summed = lax.psum(density, 'kt')]
    pallas_call x1, Pallas kernels: 18.7 us -> 90.5 us  [body(): pl.pallas_call(kernel, out_shape=(jax.ShapeDtypeStruct((slabs, n), f32),...]
    unnamed x1 -> x0, blocking collectives: 28 us -> none
    all_gather x1 -> x0, blocking collectives: 23.8 us -> none  [body(): lax.all_gather(jnp.stack([-onsite - potential_in, hopping, imag], 1), 'en...]
  transfers between devices with their start and end apart: 1 -> 0, of which waited for: 1 -> 0; matrix products, arithmetic and copies ran while one was open for 0% -> 0% of each run, Pallas kernels for 0% -> 0%
where the time goes in v2:
time: 100 us; the launch traced here: 99.6 us
  Pallas kernels  90.5 us (90%)
  local copies, waits for them, and re-layouts  6.14 us (6%)
  other arithmetic  1.49 us (1%)
  between operations  1.46 us (1%)
    pallas_call x1, Pallas kernels, body(): pl.pallas_call(kernel, out_shape=(jax.ShapeDtypeStruct((slabs, n), f32),...  90.5 us
    unnamed x12, local copies, waits for them, and re-layouts  6.14 us

profile of v2, /device:TPU:1, one launch (start us, length us, event | category | flops | bytes accessed | tf_op | source)
XLA Modules:
  0.0 99.6 jit_solution(18163134448357807909)
XLA Ops:
  1.4 0.1 pad_maximum_fusion.1.scal_ref
  1.5 0.7 negate_subtract_fusion
  2.2 0.7 pad_maximum_fusion.tab_in
  2.9 0.0 copy-start
  2.9 1.3 %copy-done = bf16[4,384,384]{2,1,0:T(8,128)(2,1)S(1)} copy-done((bf16[4,384,384]{2,1,0:T(8,128)(2,1)S(1)}, bf16[4,384,384]{2,1,0:T(8,128)(2,1)}, u32[]{:S(2)}) %copy-start) | copy-done | bytes 1179672
  4.2 0.0 copy-start.1
  4.2 1.3 %copy-done.1 = bf16[4,384,384]{2,1,0:T(8,128)(2,1)S(1)} copy-done((bf16[4,384,384]{2,1,0:T(8,128)(2,1)S(1)}, bf16[4,384,384]{2,1,0:T(8,128)(2,1)}, u32[]{:S(2)}) %copy-start.1) | copy-done | bytes 1179672
  5.5 0.0 copy-start.2
  5.5 1.1 %copy-done.2 = f32[384,384]{1,0:T(8,128)S(1)} copy-done((f32[384,384]{1,0:T(8,128)S(1)}, f32[384,384]{1,0:T(8,128)}, u32[]{:S(2)}) %copy-start.2) | copy-done | bytes 589848
  6.5 0.0 copy-start.3
  6.5 0.7 copy-done.3
  7.2 0.0 copy-start.4
  7.2 0.7 copy-done.4
  7.9 90.5 %shard_map.104 = (f32[4,384]{1,0:T(4,128)S(1)}, f32[4,384]{1,0:T(4,128)S(1)}) custom-call(f32[3]{0:T(128)S(1)} %pad_maximum_fusion.1.scal_ref, s32[2]{0:T(128)S(1)} %copy-done.4, f32[8,384]{1,0:T(8,128)S(1)} %pad_maximum_fusion.tab_in, bf16[4,384,384]{2,1,0:T(8,128)(2,1)S(1)} %copy-done, bf16[4,384,384]{2,1,0:T(8,128)(2,1)S(1)} %copy-done.1, ...), custom_call_target="tpu_custom_call" | custom-call | tf_op jit(solution)/shard_map/pallas_call | solution.py:308
  98.4 0.6 copy.14
  99.0 0.6 copy.15
Async XLA Ops:
  2.9 1.3 %copy-start = (bf16[4,384,384]{2,1,0:T(8,128)(2,1)S(1)}, bf16[4,384,384]{2,1,0:T(8,128)(2,1)}, u32[]{:S(2)}) copy-start(bf16[4,384,384]{2,1,0:T(8,128)(2,1)} %base_ref.1) | copy-start | bytes 3538948
  4.2 1.3 %copy-start.1 = (bf16[4,384,384]{2,1,0:T(8,128)(2,1)S(1)}, bf16[4,384,384]{2,1,0:T(8,128)(2,1)}, u32[]{:S(2)}) copy-start(bf16[4,384,384]{2,1,0:T(8,128)(2,1)} %wave_ref.1) | copy-start | bytes 3538948
  5.5 1.1 %copy-start.2 = (f32[384,384]{1,0:T(8,128)S(1)}, f32[384,384]{1,0:T(8,128)}, u32[]{:S(2)}) copy-start(f32[384,384]{1,0:T(8,128)} %inverse_ref.1) | copy-start | bytes 1769476
  6.5 0.7 copy-start.3
  7.2 0.7 copy-start.4

commit v3 on v1

v3 whole, which is shorter than its diff:
```python
import jax
import jax.numpy as jnp
from jax import lax
from jax.experimental import pallas as pl
from jax.experimental.pallas import tpu as pltpu
from jax.sharding import PartitionSpec as P

f32, bf16 = jnp.float32, jnp.bfloat16
NT = (((1,), (1,)), ((), ()))
MESH = pl.DeviceIdType.MESH

BOTTOM, GAP, FILLING, SPREAD = -1.0, 0.25, -0.5, 0.1
BROADENING, CONTACT = 1.0, 0.5
NX, NY, NZ, EN, CORES = 4, 4, 4, 4, 2
PLANE = NX * NY
LANES, SUB = 128, 8
SOURCES = ((4, (3, 2, 1, 0)), (8, (3, 2)), (11, (0, 1)), (15, (0, 1, 2, 3)))


def kernel(
    counts_in, contact_in, onsite_in, hopping_in, potential_in, base_ref, wave_ref, doping_in, inverse_in,
    den_out, pot_out,
    w_ref, tab_ref, tab_own, rows_ref, doping_ref, inverse_ref, counts_ref, contact_ref,
    count_in, count_mine, count_all, par_ref, g_ref, l_ref, c_ref, den_ref, plane_in, sum_ref, last_in,
    load_sems, small_sems, tab_sems, count_sems, zone_sems, z_send, z_recv, row_sems, plane_sems, chip_sems,
    sum_sems, last_send, last_recv, ready_sem,
):
    kt, e = lax.axis_index("kt"), lax.axis_index("en")
    x, y, zl, c = kt // 32, (kt // 8) % 4, (kt // 2) % 4, kt % 2
    xy = x * NY + y
    slabs, n = base_ref.shape[0], base_ref.shape[-1]
    total = slabs * EN
    pairs, own_pairs = total // CORES, slabs // CORES
    blocks = n // LANES
    part = 2 * n // PLANE

    def place(x, y, zl, c):
        return (((x % NX) * NY + y % NY) * NZ + zl % NZ) * CORES + c % CORES

    def remote(src, dst, send, recv, where):
        return pltpu.make_async_remote_copy(src, dst, send, recv, device_id=where, device_id_type=MESH)

    def rows(first, count):
        return pl.ds(pl.multiple_of(first, 16), count)

    a, b = x + c * (y - x), y + c * (x - y)
    piece_at = 4 * b + a
    barrier = pltpu.get_barrier_semaphore()

    def in_plane(d):
        return place(x + d // NY, y + d % NY, zl, c), e

    def zone(d):
        return place(x, y, zl + d // CORES, c + d % CORES), e

    small = [
        pltpu.make_async_copy(src, dst, small_sems.at[i])
        for i, (src, dst) in enumerate((
            (onsite_in, rows_ref.at[0]), (potential_in, rows_ref.at[1]), (hopping_in, rows_ref.at[2]),
            (doping_in, doping_ref), (inverse_in, inverse_ref), (counts_in, counts_ref), (contact_in, contact_ref),
        ))
    ]
    for copy in small:
        copy.start()

    def send_last(group, d):
        return remote(
            sum_ref.at[group], last_in.at[zl * CORES + c], last_send.at[group, d], last_recv.at[zl * CORES + c],
            (place(x, y, d // CORES, d % CORES), group),
        )

    def finish():
        acc = last_in[0]
        for i in range(1, NZ * CORES):
            acc = acc + last_in[i]
        pot = jnp.zeros((slabs, n), f32)
        for j in range(blocks):
            sl = slice(LANES * j, LANES * (j + 1))
            block = acc[slabs * j:slabs * (j + 1), :]
            den_out[:, sl] = block
            pot = pot + lax.dot_general(
                block - doping_ref[:, sl], inverse_ref[:, sl], NT,
                precision=lax.Precision.HIGHEST, preferred_element_type=f32,
            )
        pot_out[...] = pot

    def make_tab():
        for copy in small[:3]:
            copy.wait()
        tab_own[:slabs] = -rows_ref[0] - rows_ref[1]
        tab_own[slabs:] = rows_ref[2]

    def tab_copy(run):
        return remote(tab_own, tab_ref.at[run], tab_sems.at[0], tab_sems.at[run], (kt, 0))

    @pl.when(e != 0)
    def _():
        make_tab()
        pl.semaphore_wait(barrier, NZ * CORES)
        for d in range(NZ * CORES):
            pl.semaphore_signal(
                ready_sem, 1, device_id=(place(x, y, d // CORES, d % CORES), 0), device_id_type=MESH
            )

        def send_z(source, first, i, slot, to):
            run = source // NZ
            k = run * own_pairs + i
            local = 2 * i + c
            ref = base_ref if first else wave_ref
            index = piece_at if first else piece_at - PLANE // 2
            return remote(
                ref.at[local, rows(part * index, part)],
                w_ref.at[2 * k + c, rows(part * piece_at, part)],
                z_send.at[i, slot], z_recv.at[k], (place(x, y, to, c), 0),
            )

        for act in ("start", "wait_send"):
            for source, targets in SOURCES:
                for first in (True, False):
                    in_half = (piece_at < PLANE // 2) if first else (piece_at >= PLANE // 2)

                    @pl.when(jnp.logical_and(e * NZ + zl == source, in_half))
                    def _():
                        for i in range(own_pairs):
                            for slot, to in enumerate(targets):
                                getattr(send_z(source, first, i, slot, to), act)()

            if act == "start":
                tab_copy(e).start()
        tab_copy(e).wait_send()
        for i in range(NZ * CORES):
            remote(sum_ref.at[0], last_in.at[i], last_send.at[0, 0], last_recv.at[i], (kt, 0)).wait_recv()
        for copy in small[3:]:
            copy.wait()
        finish()

    @pl.when(e == 0)
    def _():
        def loads(i):
            return (
                pltpu.make_async_copy(base_ref.at[i], w_ref.at[i, :n], load_sems.at[0, i]),
                pltpu.make_async_copy(wave_ref.at[i], w_ref.at[i, n:], load_sems.at[1, i]),
            )

        for i in range(1, slabs):
            for copy in loads(i):
                copy.start()
        for d in range(1, PLANE):
            pl.semaphore_signal(barrier, 1, device_id=in_plane(d), device_id_type=MESH)
        for d in range(1, NZ * CORES):
            pl.semaphore_signal(barrier, 1, device_id=zone(d), device_id_type=MESH)
        for run in range(1, EN):
            for d in range(NZ * CORES):
                pl.semaphore_signal(
                    barrier, 1, device_id=(place(x, y, d // CORES, d % CORES), run), device_id_type=MESH
                )

        lane = lax.broadcasted_iota(jnp.int32, (SUB, LANES), 1)
        momentum = (lane % PLANE) * (NZ * CORES) + lane // PLANE
        cosines = jnp.cos(jnp.pi * (momentum.astype(f32) + 0.5) / (PLANE * NZ * CORES))
        me = (zl * CORES + c) * PLANE + xy

        def set_params(item, cosine, j):
            energy = BOTTOM + GAP * j
            par_ref[item, 0] = cosine
            par_ref[item, 1] = energy
            par_ref[item, 2] = GAP / (1.0 + jnp.exp((energy - FILLING) / SPREAD)) / jnp.pi

        def pick(mask, values):
            return jnp.broadcast_to(jnp.sum(jnp.where(mask, values, 0.0), axis=1, keepdims=True), (SUB, LANES))

        set_params(0, pick(lane == me, cosines), jnp.zeros((SUB, LANES), f32))
        make_tab()
        tab_ref[0] = tab_own[...]
        for copy in small[5:]:
            copy.wait()
        den_ref[...] = jnp.zeros_like(den_ref)

        eye = lax.broadcasted_iota(jnp.int32, (LANES, LANES), 0) == lax.broadcasted_iota(jnp.int32, (LANES, LANES), 1)

        def wide(item, which):
            row = par_ref[item, which, 0:1, :]
            return jnp.concatenate([row] * blocks, axis=1)

        def inverse_diag(item, s):
            group, local = s // slabs, s % slabs
            touches = jnp.logical_or(contact_ref[0] == s, contact_ref[1] == s)
            di = BROADENING + CONTACT * touches.astype(f32)
            dr = (
                wide(item, 1) + tab_ref[group, pl.ds(local, 1), :]
                - wide(item, 0) * tab_ref[group, pl.ds(slabs + local, 1), :]
            )
            mag = dr * dr + di * di
            return dr / mag, -di / mag

        def add_density(s, j, value):
            at = pl.ds(slabs * j + s % slabs, 1)
            den_ref[s // slabs, at, :] = den_ref[s // slabs, at, :] + value

        def first_slab(item):
            g = g_ref.at[item]
            g[...] = jnp.zeros_like(g)
            br, bi = inverse_diag(item, 0)
            for i in range(blocks):
                sl = slice(LANES * i, LANES * (i + 1))
                g[2 * LANES * i:2 * LANES * i + LANES, sl] = jnp.where(eye, br[:, sl], 0.0).astype(bf16)
                g[2 * LANES * i + LANES:2 * LANES * (i + 1), sl] = jnp.where(eye, bi[:, sl], 0.0).astype(bf16)
                add_density(0, i, -par_ref[item, 2, 0:1, :] * bi[:, sl])

        def couple(item, s):
            cosine = wide(item, 0)
            c_ref[item] = (w_ref[s, :n].astype(f32) + cosine * w_ref[s, n:].astype(f32)).astype(bf16)

        def left_product(item):
            for j in range(blocks):
                left = lax.dot_general(
                    c_ref[item], g_ref[item, 2 * LANES * j:2 * LANES * (j + 1), :], NT, preferred_element_type=f32
                ).astype(bf16)
                sl = slice(LANES * j, LANES * (j + 1))
                for i in range(blocks):
                    piece = left[LANES * i:LANES * (i + 1)]
                    l_ref[item, 2 * LANES * i:2 * LANES * i + LANES, sl] = piece[:, :LANES]
                    l_ref[item, 2 * LANES * i + LANES:2 * LANES * (i + 1), sl] = piece[:, LANES:]

        def green(item, s):
            br, bi = inverse_diag(item, s)
            brc = jnp.transpose(jnp.broadcast_to(br, (LANES, n)))
            bic = jnp.transpose(jnp.broadcast_to(bi, (LANES, n)))
            for j in range(blocks):
                lo = LANES * j
                sl = slice(lo, lo + LANES)
                energy_part = lax.dot_general(
                    c_ref[item, lo:, :], l_ref[item, 2 * lo:2 * lo + 2 * LANES, :], NT, preferred_element_type=f32
                )
                for i in range(j, blocks):
                    piece = energy_part[LANES * i - lo:LANES * (i + 1) - lo]
                    se_r, se_i = piece[:, :LANES], piece[:, LANES:]
                    cr, ci = brc[LANES * i:LANES * (i + 1)], bic[LANES * i:LANES * (i + 1)]
                    rr, ri = br[:, sl], bi[:, sl]
                    hr = cr * se_r - ci * se_i
                    hi = cr * se_i + ci * se_r
                    gr = hr * rr - hi * ri
                    gi = hr * ri + hi * rr
                    if i == j:
                        gr = gr + jnp.where(eye, rr, 0.0)
                        gi = gi + jnp.where(eye, ri, 0.0)
                        add_density(
                            s, j, -par_ref[item, 2, 0:1, :] * jnp.sum(jnp.where(eye, gi, 0.0), axis=0, keepdims=True)
                        )
                    gr, gi = gr.astype(bf16), gi.astype(bf16)
                    g_ref[item, 2 * LANES * i:2 * LANES * i + LANES, sl] = gr
                    g_ref[item, 2 * LANES * i + LANES:2 * LANES * (i + 1), sl] = gi
                    if i > j:
                        si = slice(LANES * i, LANES * (i + 1))
                        g_ref[item, 2 * lo:2 * lo + LANES, si] = jnp.transpose(gr)
                        g_ref[item, 2 * lo + LANES:2 * lo + 2 * LANES, si] = jnp.transpose(gi)

        def slab(items, s):
            for item in items:
                couple(item, s)
            for item in items:
                left_product(item)
            for item in items:
                green(item, s)

        def own_piece(k):
            return w_ref.at[2 * k + c, rows(part * piece_at, part)]

        def send_row(k, d):
            to = place(x + (1 - c) * d, y + c * d, zl, c), e
            return remote(own_piece(k), own_piece(k), row_sems.at[0, k, d - 1], row_sems.at[1, k, d - 1], to)

        def send_plane(k, d):
            here = w_ref.at[2 * k + c, rows(part * 4 * b, 4 * part)]
            to = place(x + c * d, y + (1 - c) * d, zl, c), e
            return remote(here, here, plane_sems.at[0, k, d - 1], plane_sems.at[1, k, d - 1], to)

        def send_chip(k):
            here = w_ref.at[2 * k + c]
            return remote(here, here, chip_sems.at[0, k], chip_sems.at[1, k], (place(x, y, zl, 1 - c), e))

        def stage_row(k):
            @pl.when(k < pairs)
            def _():
                remote(own_piece(k), own_piece(k), z_send.at[0, 0], z_recv.at[k], (kt, 1)).wait_recv()
                for d in range(1, 4):
                    send_row(k, d).start()

        def stage_plane(k):
            @pl.when(k < pairs)
            def _():
                for d in range(1, 4):
                    send_row(k, d).wait_recv()
                for d in range(1, 4):
                    send_plane(k, d).start()

        def stage_chip(k):
            @pl.when(k < pairs)
            def _():
                for d in range(1, 4):
                    send_plane(k, d).wait_recv()
                send_chip(k).start()

        def stage_here(k):
            there = w_ref.at[2 * k + 1 - c]
            remote(there, there, chip_sems.at[0, k], chip_sems.at[1, k], (place(x, y, zl, 1 - c), e)).wait_recv()

        def send_sum(group, d):
            return remote(
                den_ref.at[group], plane_in.at[group, xy], sum_sems.at[0, group, d - 1], sum_sems.at[1, group, d - 1],
                in_plane(d),
            )

        def start_sum(group):
            for d in range(1, PLANE):
                send_sum(group, d).start()
            plane_in[group, xy] = den_ref[group]

        def end_sum(group):
            for d in range(1, PLANE):
                sender = ((x - d // NY + NX) % NX) * NY + (y - d % NY + NY) % NY
                remote(
                    den_ref.at[group], plane_in.at[group, sender], sum_sems.at[0, group, d - 1],
                    sum_sems.at[1, group, d - 1], in_plane(d),
                ).wait_recv()
            acc = plane_in[group, 0]
            for i in range(1, PLANE):
                acc = acc + plane_in[group, i]
            sum_ref[group] = acc
            for d in range(NZ * CORES):
                if group == 0:
                    @pl.when(d != zl * CORES + c)
                    def _():
                        send_last(group, d).start()
                else:
                    send_last(group, d).start()

        first_slab(0)
        for i in range(1, slabs):
            for copy in loads(i):
                copy.wait()

        def alone(item):
            def step(s, carry):
                slab((item,), s)
                return carry

            return step

        lax.fori_loop(1, slabs, alone(0), 0)

        pl.semaphore_wait(barrier, PLANE - 1 + NZ * CORES - 1)
        mine = jnp.zeros((SUB, LANES), jnp.int32) + counts_ref[0]
        count_mine[0] = mine.astype(f32)

        def send_count(d):
            return remote(
                count_mine.at[0], count_in.at[xy], count_sems.at[0, d - 1], count_sems.at[1, d - 1], in_plane(d)
            )

        for d in range(1, PLANE):
            send_count(d).start()
        count_in[xy] = count_mine[0]
        for d in range(1, PLANE):
            sender = ((x - d // NY + NX) % NX) * NY + (y - d % NY + NY) % NY
            remote(
                count_mine.at[0], count_in.at[sender], count_sems.at[0, d - 1], count_sems.at[1, d - 1], in_plane(d)
            ).wait_recv()
        here = (zl * CORES + c) * PLANE
        line = jnp.zeros((SUB, LANES), f32)
        for i in range(PLANE):
            line = line + jnp.where(lane == here + i, count_in[i], 0.0)
        count_mine[1] = line

        def send_zone(d):
            return remote(
                count_mine.at[1], count_all.at[zl * CORES + c], zone_sems.at[0, d - 1], zone_sems.at[1, d - 1], zone(d)
            )

        for d in range(1, NZ * CORES):
            send_zone(d).start()
        count_all[zl * CORES + c] = line
        stage_row(own_pairs)
        stage_row(own_pairs + 1)
        stage_plane(own_pairs)
        for d in range(1, NZ * CORES):
            from_z, from_c = (zl - d // CORES + NZ) % NZ, (c + d) % CORES
            remote(
                count_mine.at[1], count_all.at[from_z * CORES + from_c], zone_sems.at[0, d - 1],
                zone_sems.at[1, d - 1], zone(d),
            ).wait_recv()
        every = count_all[0]
        for i in range(1, NZ * CORES):
            every = every + count_all[i]
        extra = every - 1.0
        upper = (
            lax.broadcasted_iota(jnp.int32, (LANES, LANES), 0) <= lax.broadcasted_iota(jnp.int32, (LANES, LANES), 1)
        )
        upto = jnp.dot(extra.astype(bf16), upper.astype(f32).astype(bf16), preferred_element_type=f32)
        before = upto - extra
        mine_f = jnp.zeros((SUB, LANES), jnp.int32) + me
        mine_f = mine_f.astype(f32)
        owner = jnp.logical_and(before <= mine_f, mine_f < upto)
        set_params(1, pick(owner, cosines), pick(owner, 1.0 + mine_f - before))
        first_slab(1)
        stage_row(own_pairs + 2)
        stage_plane(own_pairs + 1)
        slab((1,), 1)
        stage_chip(own_pairs)
        slab((1,), 2)
        stage_row(own_pairs + 3)
        stage_plane(own_pairs + 2)
        slab((1,), 3)
        start_sum(0)
        for run in range(1, EN):
            remote(tab_own, tab_ref.at[run], tab_sems.at[0], tab_sems.at[run], (kt, 0)).wait_recv()

        def both(s, carry):
            k = s // CORES

            @pl.when(s % CORES == 0)
            def _():
                stage_chip(k + 1)
                stage_here(k)

            @pl.when(s % CORES == 1)
            def _():
                stage_row(k + 4)
                stage_plane(k + 3)

            slab((0, 1), s)
            return carry

        lax.fori_loop(slabs, 2 * slabs, both, 0)
        start_sum(1)
        pl.semaphore_wait(ready_sem, (EN - 1) * NZ * CORES)
        end_sum(0)
        lax.fori_loop(2 * slabs, 3 * slabs, both, 0)
        start_sum(2)
        end_sum(1)
        lax.fori_loop(3 * slabs, 4 * slabs, both, 0)
        start_sum(3)
        end_sum(2)
        end_sum(3)

        last_in[zl * CORES + c] = sum_ref[0]
        for d in range(1, NZ * CORES):
            at = (zl * CORES + c + d) % (NZ * CORES)
            remote(sum_ref.at[0], last_in.at[at], last_send.at[0, 0], last_recv.at[at], (kt, 1)).wait_recv()
        for copy in small[3:5]:
            copy.wait()
        finish()

        for d in range(1, PLANE):
            send_count(d).wait_send()
        for d in range(1, NZ * CORES):
            send_zone(d).wait_send()

        def left(k, carry):
            for d in range(1, 4):
                send_row(k, d).wait_send()
                send_plane(k, d).wait_send()
            send_chip(k).wait_send()
            return carry

        lax.fori_loop(own_pairs, pairs, left, 0)
        for group in range(EN):
            for d in range(1, PLANE):
                send_sum(group, d).wait_send()
            for d in range(NZ * CORES):
                if group == 0:
                    @pl.when(d != zl * CORES + c)
                    def _():
                        send_last(group, d).wait_send()
                else:
                    send_last(group, d).wait_send()


def body(counts, contact_slabs, onsite, hopping, potential_in, couple_base, couple_wave, doping, poisson_inverse):
    slabs, n = onsite.shape
    total = slabs * EN
    pairs = total // CORES
    vmem, anywhere = pl.BlockSpec(memory_space=pltpu.VMEM), pl.BlockSpec(memory_space=pl.ANY)
    piece = (4 * slabs, LANES)
    tile = (SUB, LANES)
    sems = pltpu.SemaphoreType.DMA
    return pl.pallas_call(
        kernel,
        out_shape=(jax.ShapeDtypeStruct((slabs, n), f32), jax.ShapeDtypeStruct((slabs, n), f32)),
        in_specs=[anywhere] * 9,
        out_specs=(vmem, vmem),
        scratch_shapes=[
            pltpu.VMEM((total, 2 * n, n), bf16),
            pltpu.VMEM((EN, 2 * slabs, n), f32),
            pltpu.VMEM((2 * slabs, n), f32),
            pltpu.VMEM((3, slabs, n), f32),
            pltpu.VMEM((slabs, n), f32),
            pltpu.VMEM((n, n), f32),
            pltpu.SMEM((1,), jnp.int32),
            pltpu.SMEM((2,), jnp.int32),
            pltpu.VMEM((PLANE, *tile), f32),
            pltpu.VMEM((2, *tile), f32),
            pltpu.VMEM((NZ * CORES, *tile), f32),
            pltpu.VMEM((2, 3, *tile), f32),
            pltpu.VMEM((2, 2 * n, n), bf16),
            pltpu.VMEM((2, 2 * n, n), bf16),
            pltpu.VMEM((2, n, n), bf16),
            pltpu.VMEM((EN, *piece), f32),
            pltpu.VMEM((EN, PLANE, *piece), f32),
            pltpu.VMEM((EN, *piece), f32),
            pltpu.VMEM((NZ * CORES, *piece), f32),
            sems((2, slabs)),
            sems((7,)),
            sems((EN,)),
            sems((2, PLANE - 1)),
            sems((2, NZ * CORES - 1)),
            sems((slabs // CORES, NZ)),
            sems((pairs,)),
            sems((2, pairs, 3)),
            sems((2, pairs, 3)),
            sems((2, pairs)),
            sems((2, EN, PLANE - 1)),
            sems((EN, NZ * CORES)),
            sems((NZ * CORES,)),
            pltpu.SemaphoreType.REGULAR,
        ],
        compiler_params=pltpu.CompilerParams(collective_id=0, has_side_effects=True, vmem_limit_bytes=40 * 2**20),
    )(counts, contact_slabs, onsite, hopping, potential_in, couple_base, couple_wave, doping, poisson_inverse)


def solution(mesh):
    return jax.shard_map(
        body,
        mesh=mesh,
        in_specs=(
            P("kt"), P(), P("en", None), P("en", None), P("en", None),
            P("en", None, None), P("en", None, None), P("en", None), P(),
        ),
        out_specs=(P("en", None), P("en", None)),
        check_vma=False,
    )
```

time: 1840 us -> 83.4 us (0.05)
  waiting for transfers between devices: 1400 us -> 0 us
  blocking collectives: 390 us -> 0 us
  Pallas kernels: 18.7 us -> 73.5 us
    all_gather x1 -> x0, waiting for transfers between devices: 1400 us -> none  [body(): lax.all_gather(piece, ('kt', 'en'), tiled=True)]
    psum x1 -> x0, blocking collectives: 338 us -> none  [body(): summed = lax.psum(density, 'kt')]
    pallas_call x1, Pallas kernels: 18.7 us -> 73.5 us  [body(): pl.pallas_call(kernel, out_shape=(jax.ShapeDtypeStruct((slabs, n), f32),...]
    unnamed x1 -> x0, blocking collectives: 28 us -> none
    all_gather x1 -> x0, blocking collectives: 23.8 us -> none  [body(): lax.all_gather(jnp.stack([-onsite - potential_in, hopping, imag], 1), 'en...]
  transfers between devices with their start and end apart: 1 -> 0, of which waited for: 1 -> 0; matrix products, arithmetic and copies ran while one was open for 0% -> 0% of each run, Pallas kernels for 0% -> 0%
where the time goes in v3:
time: 83.4 us; the launch traced here: 83 us
  Pallas kernels  73.5 us (88%)
  local copies, waits for them, and re-layouts  8.2 us (10%)
  between operations  1.3 us (2%)
    pallas_call x1, Pallas kernels, body(): pl.pallas_call(kernel, out_shape=(jax.ShapeDtypeStruct((slabs, n), f32),...  73.5 us
    unnamed x18, local copies, waits for them, and re-layouts  8.2 us

profile of v3, /device:TPU:1, one launch (start us, length us, event | category | flops | bytes accessed | tf_op | source)
XLA Modules:
  0.0 83.0 jit_solution(4406849389270793357)
XLA Ops:
  1.3 0.0 copy-start
  1.3 1.3 %copy-done = bf16[4,384,384]{2,1,0:T(8,128)(2,1)S(1)} copy-done((bf16[4,384,384]{2,1,0:T(8,128)(2,1)S(1)}, bf16[4,384,384]{2,1,0:T(8,128)(2,1)}, u32[]{:S(2)}) %copy-start) | copy-done | bytes 1179672
  2.5 0.0 copy-start.1
  2.6 1.3 %copy-done.1 = bf16[4,384,384]{2,1,0:T(8,128)(2,1)S(1)} copy-done((bf16[4,384,384]{2,1,0:T(8,128)(2,1)S(1)}, bf16[4,384,384]{2,1,0:T(8,128)(2,1)}, u32[]{:S(2)}) %copy-start.1) | copy-done | bytes 1179672
  3.8 0.0 copy-start.2
  3.8 1.1 %copy-done.2 = f32[384,384]{1,0:T(8,128)S(1)} copy-done((f32[384,384]{1,0:T(8,128)S(1)}, f32[384,384]{1,0:T(8,128)}, u32[]{:S(2)}) %copy-start.2) | copy-done | bytes 589848
  4.9 0.0 copy-start.3
  4.9 0.7 copy-done.3
  5.6 0.0 copy-start.4
  5.6 0.7 copy-done.4
  6.3 0.0 copy-start.5
  6.3 0.7 copy-done.5
  7.0 0.0 copy-start.6
  7.0 0.7 copy-done.6
  7.7 0.0 copy-start.7
  7.7 0.7 copy-done.7
  8.3 73.5 %shard_map.104 = (f32[4,384]{1,0:T(4,128)S(1)}, f32[4,384]{1,0:T(4,128)S(1)}) custom-call(s32[1]{0:T(128)S(6)} %copy.13.counts_in, s32[2]{0:T(128)S(1)} %copy-done.7, f32[4,384]{1,0:T(4,128)S(1)} %copy-done.3, f32[4,384]{1,0:T(4,128)S(1)} %copy-done.4, f32[4,384]{1,0:T(4,128)S(1)} %copy-done.5, bf16[4,384,384]{2,1,0:T(8,128)(2,1)S(1)} %copy-done, ...), custom_call_target="tpu_custom_call" | custom-call | tf_op jit(solution)/shard_map/pallas_call | solution.py:487
  81.8 0.6 copy.14
  82.4 0.6 copy.15
Async XLA Ops:
  1.3 1.3 %copy-start = (bf16[4,384,384]{2,1,0:T(8,128)(2,1)S(1)}, bf16[4,384,384]{2,1,0:T(8,128)(2,1)}, u32[]{:S(2)}) copy-start(bf16[4,384,384]{2,1,0:T(8,128)(2,1)} %base_ref.1) | copy-start | bytes 3538948
  2.5 1.3 %copy-start.1 = (bf16[4,384,384]{2,1,0:T(8,128)(2,1)S(1)}, bf16[4,384,384]{2,1,0:T(8,128)(2,1)}, u32[]{:S(2)}) copy-start(bf16[4,384,384]{2,1,0:T(8,128)(2,1)} %wave_ref.1) | copy-start | bytes 3538948
  3.8 1.1 %copy-start.2 = (f32[384,384]{1,0:T(8,128)S(1)}, f32[384,384]{1,0:T(8,128)}, u32[]{:S(2)}) copy-start(f32[384,384]{1,0:T(8,128)} %inverse_in.1) | copy-start | bytes 1769476
  4.9 0.7 copy-start.3
  5.6 0.7 copy-start.4
  6.3 0.7 copy-start.5
  7.0 0.7 copy-start.6
  7.7 0.7 copy-start.7

commit v4 on v3

--- a/solution.py
+++ b/solution.py
@@ -7,6 +7,7 @@
 
 f32, bf16 = jnp.float32, jnp.bfloat16
 NT = (((1,), (1,)), ((), ()))
+NN = (((1,), (0,)), ((), ()))
 MESH = pl.DeviceIdType.MESH
 
 BOTTOM, GAP, FILLING, SPREAD = -1.0, 0.25, -0.5, 0.1
@@ -21,9 +22,9 @@
     counts_in, contact_in, onsite_in, hopping_in, potential_in, base_ref, wave_ref, doping_in, inverse_in,
     den_out, pot_out,
     w_ref, tab_ref, tab_own, rows_ref, doping_ref, inverse_ref, counts_ref, contact_ref,
-    count_in, count_mine, count_all, par_ref, g_ref, l_ref, c_ref, den_ref, plane_in, sum_ref, last_in,
+    count_in, count_mine, count_all, par_ref, g_ref, l_ref, c_ref, den_ref, line_in, line_ref, plane_in,
     load_sems, small_sems, tab_sems, count_sems, zone_sems, z_send, z_recv, row_sems, plane_sems, chip_sems,
-    sum_sems, last_send, last_recv, ready_sem,
+    line_send, line_recv, sum_sems, ready_sem,
 ):
     kt, e = lax.axis_index("kt"), lax.axis_index("en")
     x, y, zl, c = kt // 32, (kt // 8) % 4, (kt // 2) % 4, kt % 2
@@ -63,26 +64,50 @@
     for copy in small:
         copy.start()
 
-    def send_last(group, d):
-        return remote(
-            sum_ref.at[group], last_in.at[zl * CORES + c], last_send.at[group, d], last_recv.at[zl * CORES + c],
-            (place(x, y, d // CORES, d % CORES), group),
-        )
+    spot = zl * CORES + c
+
+    def signal_plane():
+        for d in range(1, PLANE):
+            pl.semaphore_signal(barrier, 1, device_id=in_plane(d), device_id_type=MESH)
+
+    def send_plane_sum(d):
+        return remote(line_ref, plane_in.at[xy], sum_sems.at[0, d - 1], sum_sems.at[1, d - 1], in_plane(d))
+
+    def sum_line(first):
+        for d in range(first, NZ * CORES):
+            at = (spot + d) % (NZ * CORES)
+            remote(line_ref, line_in.at[at], line_send.at[0, 0], line_recv.at[at], (kt, 0)).wait_recv()
+        acc = line_in[0]
+        for i in range(1, NZ * CORES):
+            acc = acc + line_in[i]
+        line_ref[...] = acc
+        plane_in[xy] = acc
+        for d in range(1, PLANE):
+            send_plane_sum(d).start()
 
     def finish():
-        acc = last_in[0]
-        for i in range(1, NZ * CORES):
-            acc = acc + last_in[i]
+        for copy in small[3:5]:
+            copy.wait()
+        for d in range(1, PLANE):
+            sender = ((x - d // NY + NX) % NX) * NY + (y - d % NY + NY) % NY
+            remote(line_ref, plane_in.at[sender], sum_sems.at[0, d - 1], sum_sems.at[1, d - 1], in_plane(d)).wait_recv()
+        acc = plane_in[0]
+        for i in range(1, PLANE):
+            acc = acc + plane_in[i]
         pot = jnp.zeros((slabs, n), f32)
         for j in range(blocks):
             sl = slice(LANES * j, LANES * (j + 1))
-            block = acc[slabs * j:slabs * (j + 1), :]
+            block = jnp.concatenate(
+                [acc[i // CORES, blocks * (i % CORES) + j:blocks * (i % CORES) + j + 1] for i in range(slabs)], axis=0
+            )
             den_out[:, sl] = block
             pot = pot + lax.dot_general(
                 block - doping_ref[:, sl], inverse_ref[:, sl], NT,
                 precision=lax.Precision.HIGHEST, preferred_element_type=f32,
             )
         pot_out[...] = pot
+        for d in range(1, PLANE):
+            send_plane_sum(d).wait_send()
 
     def make_tab():
         for copy in small[:3]:
@@ -95,12 +120,8 @@
 
     @pl.when(e != 0)
     def _():
-        make_tab()
-        pl.semaphore_wait(barrier, NZ * CORES)
-        for d in range(NZ * CORES):
-            pl.semaphore_signal(
-                ready_sem, 1, device_id=(place(x, y, d // CORES, d % CORES), 0), device_id_type=MESH
-            )
+        signal_plane()
+        pl.semaphore_wait(barrier, NZ * CORES + PLANE - 1)
 
         def send_z(source, first, i, slot, to):
             run = source // NZ
@@ -126,12 +147,16 @@
                                 getattr(send_z(source, first, i, slot, to), act)()
 
             if act == "start":
+                make_tab()
                 tab_copy(e).start()
+                for d in range(NZ * CORES):
+                    pl.semaphore_signal(
+                        ready_sem, 1, device_id=(place(x, y, d // CORES, d % CORES), 0), device_id_type=MESH
+                    )
         tab_copy(e).wait_send()
-        for i in range(NZ * CORES):
-            remote(sum_ref.at[0], last_in.at[i], last_send.at[0, 0], last_recv.at[i], (kt, 0)).wait_recv()
-        for copy in small[3:]:
+        for copy in small[5:]:
             copy.wait()
+        sum_line(0)
         finish()
 
     @pl.when(e == 0)
@@ -145,8 +170,7 @@
         for i in range(1, slabs):
             for copy in loads(i):
                 copy.start()
-        for d in range(1, PLANE):
-            pl.semaphore_signal(barrier, 1, device_id=in_plane(d), device_id_type=MESH)
+        signal_plane()
         for d in range(1, NZ * CORES):
             pl.semaphore_signal(barrier, 1, device_id=zone(d), device_id_type=MESH)
         for run in range(1, EN):
@@ -194,8 +218,8 @@
             return dr / mag, -di / mag
 
         def add_density(s, j, value):
-            at = pl.ds(slabs * j + s % slabs, 1)
-            den_ref[s // slabs, at, :] = den_ref[s // slabs, at, :] + value
+            at = pl.ds(blocks * (s % CORES) + j, 1)
+            den_ref[s // CORES, at, :] = den_ref[s // CORES, at, :] + value
 
         def first_slab(item):
             g = g_ref.at[item]
@@ -203,8 +227,8 @@
             br, bi = inverse_diag(item, 0)
             for i in range(blocks):
                 sl = slice(LANES * i, LANES * (i + 1))
-                g[2 * LANES * i:2 * LANES * i + LANES, sl] = jnp.where(eye, br[:, sl], 0.0).astype(bf16)
-                g[2 * LANES * i + LANES:2 * LANES * (i + 1), sl] = jnp.where(eye, bi[:, sl], 0.0).astype(bf16)
+                g[sl, 2 * LANES * i:2 * LANES * i + LANES] = jnp.where(eye, br[:, sl], 0.0).astype(bf16)
+                g[sl, 2 * LANES * i + LANES:2 * LANES * (i + 1)] = jnp.where(eye, bi[:, sl], 0.0).astype(bf16)
                 add_density(0, i, -par_ref[item, 2, 0:1, :] * bi[:, sl])
 
         def couple(item, s):
@@ -214,7 +238,7 @@
         def left_product(item):
             for j in range(blocks):
                 left = lax.dot_general(
-                    c_ref[item], g_ref[item, 2 * LANES * j:2 * LANES * (j + 1), :], NT, preferred_element_type=f32
+                    c_ref[item], g_ref[item, :, 2 * LANES * j:2 * LANES * (j + 1)], NN, preferred_element_type=f32
                 ).astype(bf16)
                 sl = slice(LANES * j, LANES * (j + 1))
                 for i in range(blocks):
@@ -248,18 +272,20 @@
                             s, j, -par_ref[item, 2, 0:1, :] * jnp.sum(jnp.where(eye, gi, 0.0), axis=0, keepdims=True)
                         )
                     gr, gi = gr.astype(bf16), gi.astype(bf16)
-                    g_ref[item, 2 * LANES * i:2 * LANES * i + LANES, sl] = gr
-                    g_ref[item, 2 * LANES * i + LANES:2 * LANES * (i + 1), sl] = gi
+                    si = slice(LANES * i, LANES * (i + 1))
+                    g_ref[item, si, 2 * lo:2 * lo + LANES] = gr
+                    g_ref[item, si, 2 * lo + LANES:2 * lo + 2 * LANES] = gi
                     if i > j:
-                        si = slice(LANES * i, LANES * (i + 1))
-                        g_ref[item, 2 * lo:2 * lo + LANES, si] = jnp.transpose(gr)
-                        g_ref[item, 2 * lo + LANES:2 * lo + 2 * LANES, si] = jnp.transpose(gi)
-
-        def slab(items, s):
+                        g_ref[item, sl, 2 * LANES * i:2 * LANES * i + LANES] = jnp.transpose(gr)
+                        g_ref[item, sl, 2 * LANES * i + LANES:2 * LANES * (i + 1)] = jnp.transpose(gi)
+
+        def slab(items, s, between=None):
             for item in items:
                 couple(item, s)
             for item in items:
                 left_product(item)
+            if between is not None:
+                between()
             for item in items:
                 green(item, s)
 
@@ -305,35 +331,20 @@
             there = w_ref.at[2 * k + 1 - c]
             remote(there, there, chip_sems.at[0, k], chip_sems.at[1, k], (place(x, y, zl, 1 - c), e)).wait_recv()
 
-        def send_sum(group, d):
+        def send_line(group, first, count, d):
+            pairs_sent = pl.ds(first, count)
+            own = first - group * own_pairs
             return remote(
-                den_ref.at[group], plane_in.at[group, xy], sum_sems.at[0, group, d - 1], sum_sems.at[1, group, d - 1],
-                in_plane(d),
-            )
-
-        def start_sum(group):
-            for d in range(1, PLANE):
-                send_sum(group, d).start()
-            plane_in[group, xy] = den_ref[group]
-
-        def end_sum(group):
-            for d in range(1, PLANE):
-                sender = ((x - d // NY + NX) % NX) * NY + (y - d % NY + NY) % NY
-                remote(
-                    den_ref.at[group], plane_in.at[group, sender], sum_sems.at[0, group, d - 1],
-                    sum_sems.at[1, group, d - 1], in_plane(d),
-                ).wait_recv()
-            acc = plane_in[group, 0]
-            for i in range(1, PLANE):
-                acc = acc + plane_in[group, i]
-            sum_ref[group] = acc
-            for d in range(NZ * CORES):
-                if group == 0:
-                    @pl.when(d != zl * CORES + c)
-                    def _():
-                        send_last(group, d).start()
-                else:
-                    send_last(group, d).start()
+                den_ref.at[pairs_sent], line_in.at[spot, pl.ds(own, count)], line_send.at[first, d], line_recv.at[spot],
+                (place(x, y, d // CORES, d % CORES), group),
+            )
+
+        def send_zone_line(d):
+            return remote(
+                den_ref.at[pl.ds(0, own_pairs)], line_in.at[spot], line_send.at[0, d], line_recv.at[spot], zone(d)
+            )
+
+        parcels = {3: (1, 2, 2), 5: (2, 4, 2), 6: (3, 6, 1), 7: (3, 7, 1)}
 
         first_slab(0)
         for i in range(1, slabs):
@@ -361,12 +372,13 @@
         for d in range(1, PLANE):
             send_count(d).start()
         count_in[xy] = count_mine[0]
+        stage_row(own_pairs)
         for d in range(1, PLANE):
             sender = ((x - d // NY + NX) % NX) * NY + (y - d % NY + NY) % NY
             remote(
                 count_mine.at[0], count_in.at[sender], count_sems.at[0, d - 1], count_sems.at[1, d - 1], in_plane(d)
             ).wait_recv()
-        here = (zl * CORES + c) * PLANE
+        here = spot * PLANE
         line = jnp.zeros((SUB, LANES), f32)
         for i in range(PLANE):
             line = line + jnp.where(lane == here + i, count_in[i], 0.0)
@@ -374,13 +386,12 @@
 
         def send_zone(d):
             return remote(
-                count_mine.at[1], count_all.at[zl * CORES + c], zone_sems.at[0, d - 1], zone_sems.at[1, d - 1], zone(d)
+                count_mine.at[1], count_all.at[spot], zone_sems.at[0, d - 1], zone_sems.at[1, d - 1], zone(d)
             )
 
         for d in range(1, NZ * CORES):
             send_zone(d).start()
-        count_all[zl * CORES + c] = line
-        stage_row(own_pairs)
+        count_all[spot] = line
         stage_row(own_pairs + 1)
         stage_plane(own_pairs)
         for d in range(1, NZ * CORES):
@@ -398,63 +409,52 @@
         )
         upto = jnp.dot(extra.astype(bf16), upper.astype(f32).astype(bf16), preferred_element_type=f32)
         before = upto - extra
-        mine_f = jnp.zeros((SUB, LANES), jnp.int32) + me
-        mine_f = mine_f.astype(f32)
+        mine_f = (jnp.zeros((SUB, LANES), jnp.int32) + me).astype(f32)
         owner = jnp.logical_and(before <= mine_f, mine_f < upto)
         set_params(1, pick(owner, cosines), pick(owner, 1.0 + mine_f - before))
         first_slab(1)
-        stage_row(own_pairs + 2)
         stage_plane(own_pairs + 1)
         slab((1,), 1)
+        stage_row(own_pairs + 2)
+        slab((1,), 2)
         stage_chip(own_pairs)
-        slab((1,), 2)
         stage_row(own_pairs + 3)
-        stage_plane(own_pairs + 2)
         slab((1,), 3)
-        start_sum(0)
+        stage_row(own_pairs + 4)
+        for d in range(1, NZ * CORES):
+            send_zone_line(d).start()
+        line_in[spot] = den_ref[:own_pairs]
         for run in range(1, EN):
             remote(tab_own, tab_ref.at[run], tab_sems.at[0], tab_sems.at[run], (kt, 0)).wait_recv()
-
-        def both(s, carry):
-            k = s // CORES
-
-            @pl.when(s % CORES == 0)
+        pl.semaphore_wait(ready_sem, (EN - 1) * NZ * CORES)
+        stage_plane(own_pairs + 2)
+
+        def both(k, carry):
+            stage_here(k)
+            stage_plane(k + 3)
+            slab((0, 1), CORES * k, lambda: stage_chip(k + 1))
+            stage_row(k + 5)
+            slab((0, 1), CORES * k + 1)
+            for last, parcel in parcels.items():
+                @pl.when(k == last)
+                def _():
+                    for d in range(NZ * CORES):
+                        send_line(*parcel, d).start()
+
+            @pl.when(k == own_pairs + 2)
             def _():
-                stage_chip(k + 1)
-                stage_here(k)
-
-            @pl.when(s % CORES == 1)
-            def _():
-                stage_row(k + 4)
-                stage_plane(k + 3)
-
-            slab((0, 1), s)
+                sum_line(1)
+
             return carry
 
-        lax.fori_loop(slabs, 2 * slabs, both, 0)
-        start_sum(1)
-        pl.semaphore_wait(ready_sem, (EN - 1) * NZ * CORES)
-        end_sum(0)
-        lax.fori_loop(2 * slabs, 3 * slabs, both, 0)
-        start_sum(2)
-        end_sum(1)
-        lax.fori_loop(3 * slabs, 4 * slabs, both, 0)
-        start_sum(3)
-        end_sum(2)
-        end_sum(3)
-
-        last_in[zl * CORES + c] = sum_ref[0]
-        for d in range(1, NZ * CORES):
-            at = (zl * CORES + c + d) % (NZ * CORES)
-            remote(sum_ref.at[0], last_in.at[at], last_send.at[0, 0], last_recv.at[at], (kt, 1)).wait_recv()
-        for copy in small[3:5]:
-            copy.wait()
+        lax.fori_loop(own_pairs, pairs, both, 0)
         finish()
 
         for d in range(1, PLANE):
             send_count(d).wait_send()
         for d in range(1, NZ * CORES):
             send_zone(d).wait_send()
+            send_zone_line(d).wait_send()
 
         def left(k, carry):
             for d in range(1, 4):
@@ -464,16 +464,9 @@
             return carry
 
         lax.fori_loop(own_pairs, pairs, left, 0)
-        for group in range(EN):
-            for d in range(1, PLANE):
-                send_sum(group, d).wait_send()
+        for parcel in parcels.values():
             for d in range(NZ * CORES):
-                if group == 0:
-                    @pl.when(d != zl * CORES + c)
-                    def _():
-                        send_last(group, d).wait_send()
-                else:
-                    send_last(group, d).wait_send()
+                send_line(*parcel, d).wait_send()
 
 
 def body(counts, contact_slabs, onsite, hopping, potential_in, couple_base, couple_wave, doping, poisson_inverse):
@@ -481,7 +474,6 @@
     total = slabs * EN
     pairs = total // CORES
     vmem, anywhere = pl.BlockSpec(memory_space=pltpu.VMEM), pl.BlockSpec(memory_space=pl.ANY)
-    piece = (4 * slabs, LANES)
     tile = (SUB, LANES)
     sems = pltpu.SemaphoreType.DMA
     return pl.pallas_call(
@@ -502,13 +494,13 @@
             pltpu.VMEM((2, *tile), f32),
             pltpu.VMEM((NZ * CORES, *tile), f32),
             pltpu.VMEM((2, 3, *tile), f32),
-            pltpu.VMEM((2, 2 * n, n), bf16),
+            pltpu.VMEM((2, n, 2 * n), bf16),
             pltpu.VMEM((2, 2 * n, n), bf16),
             pltpu.VMEM((2, n, n), bf16),
-            pltpu.VMEM((EN, *piece), f32),
-            pltpu.VMEM((EN, PLANE, *piece), f32),
-            pltpu.VMEM((EN, *piece), f32),
-            pltpu.VMEM((NZ * CORES, *piece), f32),
+            pltpu.VMEM((pairs, *tile), f32),
+            pltpu.VMEM((NZ * CORES, slabs // CORES, *tile), f32),
+            pltpu.VMEM((slabs // CORES, *tile), f32),
+            pltpu.VMEM((PLANE, slabs // CORES, *tile), f32),
             sems((2, slabs)),
             sems((7,)),
             sems((EN,)),
@@ -519,12 +511,12 @@
             sems((2, pairs, 3)),
             sems((2, pairs, 3)),
             sems((2, pairs)),
-            sems((2, EN, PLANE - 1)),
-            sems((EN, NZ * CORES)),
+            sems((pairs, NZ * CORES)),
             sems((NZ * CORES,)),
+            sems((2, PLANE - 1)),
             pltpu.SemaphoreType.REGULAR,
         ],
-        compiler_params=pltpu.CompilerParams(collective_id=0, has_side_effects=True, vmem_limit_bytes=40 * 2**20),
+        compiler_params=pltpu.CompilerParams(collective_id=0, has_side_effects=True, vmem_limit_bytes=62 * 2**20),
     )(counts, contact_slabs, onsite, hopping, potential_in, couple_base, couple_wave, doping, poisson_inverse)
 
 

time: 83.4 us -> 68.5 us (0.82)
  the two profiles are of different devices: /device:TPU:1 before, /device:TPU:384 now
where the time goes in v4:
time: 68.5 us; the launch traced here: 68.3 us
  Pallas kernels  64.4 us (94%)
  local copies, waits for them, and re-layouts  2.57 us (4%)
  between operations  1.29 us (2%)
    pallas_call x1, Pallas kernels, body(): pl.pallas_call(kernel, out_shape=(jax.ShapeDtypeStruct((slabs, n), f32),...  64.4 us
    unnamed x2, local copies, waits for them, and re-layouts  2.57 us

profile of v4, /device:TPU:384, one launch (start us, length us, event | category | flops | bytes accessed | tf_op | source)
XLA Modules:
  0.0 68.3 jit_solution(11422307471301527361)
XLA Ops:
  1.3 64.4 %shard_map.104 = (f32[4,384]{1,0:T(4,128)}, f32[4,384]{1,0:T(4,128)}) custom-call(s32[1]{0:T(128)S(6)} %copy.13.counts_in, s32[2]{0:T(128)} %contact_in.1, f32[4,384]{1,0:T(4,128)} %onsite_in.1, f32[4,384]{1,0:T(4,128)} %hopping_in.1, f32[4,384]{1,0:T(4,128)} %potential_in.1, bf16[4,384,384]{2,1,0:T(8,128)(2,1)} %base_ref.1, bf16[4,384,384]{2,1,0:T(8,128)(2,1)} %wave_ref.1, ...), custom_call_target="tpu_custom_call" | custom-call | tf_op jit(solution)/shard_map/pallas_call | solution.py:479
  65.7 1.3 %copy.14 = f32[4,384]{1,0:T(4,128)} copy(f32[4,384]{1,0:T(4,128)} %get-tuple-element.4) | data formatting | bytes 12288
  67.0 1.3 %copy.15 = f32[4,384]{1,0:T(4,128)} copy(f32[4,384]{1,0:T(4,128)} %get-tuple-element.5) | data formatting | bytes 12288

commit v5 on v4

--- a/solution.py
+++ b/solution.py
@@ -15,7 +15,7 @@
 NX, NY, NZ, EN, CORES = 4, 4, 4, 4, 2
 PLANE = NX * NY
 LANES, SUB = 128, 8
-SOURCES = ((4, (3, 2, 1, 0)), (8, (3, 2)), (11, (0, 1)), (15, (0, 1, 2, 3)))
+SOURCES = ((4, (0, 1, 2, 3)), (8, (2, 3)), (11, (1, 0)), (15, (3, 2, 1, 0)))
 
 
 def kernel(
@@ -24,7 +24,7 @@
     w_ref, tab_ref, tab_own, rows_ref, doping_ref, inverse_ref, counts_ref, contact_ref,
     count_in, count_mine, count_all, par_ref, g_ref, l_ref, c_ref, den_ref, line_in, line_ref, plane_in,
     load_sems, small_sems, tab_sems, count_sems, zone_sems, z_send, z_recv, row_sems, plane_sems, chip_sems,
-    line_send, line_recv, sum_sems, ready_sem,
+    line_send, line_recv, sum_sems, ready_sem, plane_ready,
 ):
     kt, e = lax.axis_index("kt"), lax.axis_index("en")
     x, y, zl, c = kt // 32, (kt // 8) % 4, (kt // 2) % 4, kt % 2
@@ -53,6 +53,14 @@
 
     def zone(d):
         return place(x, y, zl + d // CORES, c + d % CORES), e
+
+    @pl.when(e == 0)
+    def _():
+        for run in range(1, EN):
+            for d in range(NZ * CORES):
+                pl.semaphore_signal(
+                    barrier, 1, device_id=(place(x, y, d // CORES, d % CORES), run), device_id_type=MESH
+                )
 
     small = [
         pltpu.make_async_copy(src, dst, small_sems.at[i])
@@ -120,39 +128,50 @@
 
     @pl.when(e != 0)
     def _():
-        signal_plane()
-        pl.semaphore_wait(barrier, NZ * CORES + PLANE - 1)
-
-        def send_z(source, first, i, slot, to):
-            run = source // NZ
-            k = run * own_pairs + i
-            local = 2 * i + c
+        def fetch(i, first):
+            index = piece_at if first else piece_at - PLANE // 2
             ref = base_ref if first else wave_ref
-            index = piece_at if first else piece_at - PLANE // 2
-            return remote(
-                ref.at[local, rows(part * index, part)],
-                w_ref.at[2 * k + c, rows(part * piece_at, part)],
-                z_send.at[i, slot], z_recv.at[k], (place(x, y, to, c), 0),
-            )
-
-        for act in ("start", "wait_send"):
+            return pltpu.make_async_copy(
+                ref.at[2 * i + c, rows(part * index, part)],
+                w_ref.at[2 * (e * own_pairs + i) + c, rows(part * piece_at, part)],
+                load_sems.at[0, i],
+            )
+
+        for act in ("start", "wait"):
+            for first in (True, False):
+                in_half = (piece_at < PLANE // 2) if first else (piece_at >= PLANE // 2)
+
+                @pl.when(in_half)
+                def _():
+                    for i in range(own_pairs):
+                        getattr(fetch(i, first), act)()
+
+            if act == "start":
+                pl.semaphore_wait(barrier, NZ * CORES)
+
+        def send_z(source, i, slot, to):
+            k = source // NZ * own_pairs + i
+            here = w_ref.at[2 * k + c, rows(part * piece_at, part)]
+            return remote(here, here, z_send.at[i, slot], z_recv.at[k], (place(x, y, to, c), 0))
+
+        def act_z(i, act):
             for source, targets in SOURCES:
-                for first in (True, False):
-                    in_half = (piece_at < PLANE // 2) if first else (piece_at >= PLANE // 2)
-
-                    @pl.when(jnp.logical_and(e * NZ + zl == source, in_half))
-                    def _():
-                        for i in range(own_pairs):
-                            for slot, to in enumerate(targets):
-                                getattr(send_z(source, first, i, slot, to), act)()
-
-            if act == "start":
-                make_tab()
-                tab_copy(e).start()
-                for d in range(NZ * CORES):
-                    pl.semaphore_signal(
-                        ready_sem, 1, device_id=(place(x, y, d // CORES, d % CORES), 0), device_id_type=MESH
-                    )
+                @pl.when(e * NZ + zl == source)
+                def _():
+                    for slot, to in enumerate(targets):
+                        getattr(send_z(source, i, slot, to), act)()
+
+        for i in range(own_pairs):
+            act_z(i, "start")
+        make_tab()
+        tab_copy(e).start()
+        for d in range(NZ * CORES):
+            pl.semaphore_signal(
+                ready_sem, 1, device_id=(place(x, y, d // CORES, d % CORES), 0), device_id_type=MESH
+            )
+        for i in range(own_pairs):
+            act_z(i, "wait_send")
+
         tab_copy(e).wait_send()
         for copy in small[5:]:
             copy.wait()
@@ -173,11 +192,6 @@
         signal_plane()
         for d in range(1, NZ * CORES):
             pl.semaphore_signal(barrier, 1, device_id=zone(d), device_id_type=MESH)
-        for run in range(1, EN):
-            for d in range(NZ * CORES):
-                pl.semaphore_signal(
-                    barrier, 1, device_id=(place(x, y, d // CORES, d % CORES), run), device_id_type=MESH
-                )
 
         lane = lax.broadcasted_iota(jnp.int32, (SUB, LANES), 1)
         momentum = (lane % PLANE) * (NZ * CORES) + lane // PLANE
@@ -309,7 +323,7 @@
             @pl.when(k < pairs)
             def _():
                 remote(own_piece(k), own_piece(k), z_send.at[0, 0], z_recv.at[k], (kt, 1)).wait_recv()
-                for d in range(1, 4):
+                for d in (2, 1, 3):
                     send_row(k, d).start()
 
         def stage_plane(k):
@@ -317,7 +331,7 @@
             def _():
                 for d in range(1, 4):
                     send_row(k, d).wait_recv()
-                for d in range(1, 4):
+                for d in (2, 1, 3):
                     send_plane(k, d).start()
 
         def stage_chip(k):
@@ -326,6 +340,15 @@
                 for d in range(1, 4):
                     send_plane(k, d).wait_recv()
                 send_chip(k).start()
+
+        def send_block(k, behind):
+            here = w_ref.at[2 * k + c, rows(part * 4 * ((b + 4 - behind) % 4), 4 * part)]
+            return remote(here, here, chip_sems.at[0, k], chip_sems.at[1, k], (place(x, y, zl, 1 - c), e))
+
+        def stage_blocks(k):
+            for d in (1, 3, 2):
+                send_plane(k, d).wait_recv()
+                send_block(k, d).start()
 
         def stage_here(k):
             there = w_ref.at[2 * k + 1 - c]
@@ -394,6 +417,7 @@
         count_all[spot] = line
         stage_row(own_pairs + 1)
         stage_plane(own_pairs)
+        send_block(own_pairs, 0).start()
         for d in range(1, NZ * CORES):
             from_z, from_c = (zl - d // CORES + NZ) % NZ, (c + d) % CORES
             remote(
@@ -417,7 +441,7 @@
         slab((1,), 1)
         stage_row(own_pairs + 2)
         slab((1,), 2)
-        stage_chip(own_pairs)
+        stage_blocks(own_pairs)
         stage_row(own_pairs + 3)
         slab((1,), 3)
         stage_row(own_pairs + 4)
@@ -427,6 +451,8 @@
         for run in range(1, EN):
             remote(tab_own, tab_ref.at[run], tab_sems.at[0], tab_sems.at[run], (kt, 0)).wait_recv()
         pl.semaphore_wait(ready_sem, (EN - 1) * NZ * CORES)
+        for d in range(1, PLANE):
+            pl.semaphore_signal(plane_ready, 1, device_id=in_plane(d), device_id_type=MESH)
         stage_plane(own_pairs + 2)
 
         def both(k, carry):
@@ -435,6 +461,10 @@
             slab((0, 1), CORES * k, lambda: stage_chip(k + 1))
             stage_row(k + 5)
             slab((0, 1), CORES * k + 1)
+            @pl.when(k == own_pairs)
+            def _():
+                pl.semaphore_wait(plane_ready, PLANE - 1)
+
             for last, parcel in parcels.items():
                 @pl.when(k == last)
                 def _():
@@ -515,6 +545,7 @@
             sems((NZ * CORES,)),
             sems((2, PLANE - 1)),
             pltpu.SemaphoreType.REGULAR,
+            pltpu.SemaphoreType.REGULAR,
         ],
         compiler_params=pltpu.CompilerParams(collective_id=0, has_side_effects=True, vmem_limit_bytes=62 * 2**20),
     )(counts, contact_slabs, onsite, hopping, potential_in, couple_base, couple_wave, doping, poisson_inverse)

time: 68.5 us -> 66.3 us (0.968)
  Pallas kernels: 64.4 us -> 62.1 us
    pallas_call x1, Pallas kernels: 64.4 us -> 62.1 us  [body(): pl.pallas_call(kernel, out_shape=(jax.ShapeDtypeStruct((slabs, n), f32),...]
where the time goes in v5:
time: 66.3 us; the launch traced here: 65.9 us
  Pallas kernels  62.1 us (94%)
  local copies, waits for them, and re-layouts  2.57 us (4%)
  between operations  1.29 us (2%)
    pallas_call x1, Pallas kernels, body(): pl.pallas_call(kernel, out_shape=(jax.ShapeDtypeStruct((slabs, n), f32),...  62.1 us
    unnamed x2, local copies, waits for them, and re-layouts  2.57 us

profile of v5, /device:TPU:384, one launch (start us, length us, event | category | flops | bytes accessed | tf_op | source)
XLA Modules:
  0.0 65.9 jit_solution(16650856147675904568)
XLA Ops:
  1.3 62.1 %shard_map.104 = (f32[4,384]{1,0:T(4,128)}, f32[4,384]{1,0:T(4,128)}) custom-call(s32[1]{0:T(128)S(6)} %copy.13.counts_in, s32[2]{0:T(128)} %contact_in.1, f32[4,384]{1,0:T(4,128)} %onsite_in.1, f32[4,384]{1,0:T(4,128)} %hopping_in.1, f32[4,384]{1,0:T(4,128)} %potential_in.1, bf16[4,384,384]{2,1,0:T(8,128)(2,1)} %base_ref.1, bf16[4,384,384]{2,1,0:T(8,128)(2,1)} %wave_ref.1, ...), custom_call_target="tpu_custom_call" | custom-call | tf_op jit(solution)/shard_map/pallas_call | solution.py:509
  63.4 1.3 %copy.14 = f32[4,384]{1,0:T(4,128)} copy(f32[4,384]{1,0:T(4,128)} %get-tuple-element.4) | data formatting | bytes 12288
  64.7 1.3 %copy.15 = f32[4,384]{1,0:T(4,128)} copy(f32[4,384]{1,0:T(4,128)} %get-tuple-element.5) | data formatting | bytes 12288

commit v6 on v5

--- a/solution.py
+++ b/solution.py
@@ -20,7 +20,7 @@
 
 def kernel(
     counts_in, contact_in, onsite_in, hopping_in, potential_in, base_ref, wave_ref, doping_in, inverse_in,
-    den_out, pot_out,
+    out_ref,
     w_ref, tab_ref, tab_own, rows_ref, doping_ref, inverse_ref, counts_ref, contact_ref,
     count_in, count_mine, count_all, par_ref, g_ref, l_ref, c_ref, den_ref, line_in, line_ref, plane_in,
     load_sems, small_sems, tab_sems, count_sems, zone_sems, z_send, z_recv, row_sems, plane_sems, chip_sems,
@@ -108,12 +108,12 @@
             block = jnp.concatenate(
                 [acc[i // CORES, blocks * (i % CORES) + j:blocks * (i % CORES) + j + 1] for i in range(slabs)], axis=0
             )
-            den_out[:, sl] = block
+            out_ref[:slabs, sl] = block
             pot = pot + lax.dot_general(
                 block - doping_ref[:, sl], inverse_ref[:, sl], NT,
                 precision=lax.Precision.HIGHEST, preferred_element_type=f32,
             )
-        pot_out[...] = pot
+        out_ref[slabs:] = pot
         for d in range(1, PLANE):
             send_plane_sum(d).wait_send()
 
@@ -161,8 +161,7 @@
                     for slot, to in enumerate(targets):
                         getattr(send_z(source, i, slot, to), act)()
 
-        for i in range(own_pairs):
-            act_z(i, "start")
+        act_z(0, "start")
         make_tab()
         tab_copy(e).start()
         for d in range(NZ * CORES):
@@ -171,6 +170,9 @@
             )
         for i in range(own_pairs):
             act_z(i, "wait_send")
+            if i + 1 < own_pairs:
+                act_z(i + 1, "start")
+
 
         tab_copy(e).wait_send()
         for copy in small[5:]:
@@ -395,7 +397,6 @@
         for d in range(1, PLANE):
             send_count(d).start()
         count_in[xy] = count_mine[0]
-        stage_row(own_pairs)
         for d in range(1, PLANE):
             sender = ((x - d // NY + NX) % NX) * NY + (y - d % NY + NY) % NY
             remote(
@@ -415,6 +416,7 @@
         for d in range(1, NZ * CORES):
             send_zone(d).start()
         count_all[spot] = line
+        stage_row(own_pairs)
         stage_row(own_pairs + 1)
         stage_plane(own_pairs)
         send_block(own_pairs, 0).start()
@@ -506,11 +508,11 @@
     vmem, anywhere = pl.BlockSpec(memory_space=pltpu.VMEM), pl.BlockSpec(memory_space=pl.ANY)
     tile = (SUB, LANES)
     sems = pltpu.SemaphoreType.DMA
-    return pl.pallas_call(
+    out = pl.pallas_call(
         kernel,
-        out_shape=(jax.ShapeDtypeStruct((slabs, n), f32), jax.ShapeDtypeStruct((slabs, n), f32)),
+        out_shape=jax.ShapeDtypeStruct((2 * slabs, n), f32),
         in_specs=[anywhere] * 9,
-        out_specs=(vmem, vmem),
+        out_specs=vmem,
         scratch_shapes=[
             pltpu.VMEM((total, 2 * n, n), bf16),
             pltpu.VMEM((EN, 2 * slabs, n), f32),
@@ -549,6 +551,7 @@
         ],
         compiler_params=pltpu.CompilerParams(collective_id=0, has_side_effects=True, vmem_limit_bytes=62 * 2**20),
     )(counts, contact_slabs, onsite, hopping, potential_in, couple_base, couple_wave, doping, poisson_inverse)
+    return out[:slabs], out[slabs:]
 
 
 def solution(mesh):

time: 66.3 us -> 65 us (0.980)
  local copies, waits for them, and re-layouts: 2.57 us -> 1.38 us
    unnamed x2 -> x0, local copies, waits for them, and re-layouts: 2.57 us -> none
    slice x0 -> x1, local copies, waits for them, and re-layouts: none -> 1.38 us  [body(): return (out[:slabs], out[slabs:])]
where the time goes in v6:
time: 65 us; the launch traced here: 64.7 us
  Pallas kernels  62 us (95%)
  local copies, waits for them, and re-layouts  1.38 us (2%)
  between operations  1.29 us (2%)
    pallas_call x1, Pallas kernels, body(): pl.pallas_call(kernel, out_shape=jax.ShapeDtypeStruct((2 * slabs, n), f32...  62 us
    slice x1, local copies, waits for them, and re-layouts, body(): return (out[:slabs], out[slabs:])  1.38 us

profile of v6, /device:TPU:384, one launch (start us, length us, event | category | flops | bytes accessed | tf_op | source)
XLA Modules:
  0.0 64.7 jit_solution(15282916619269524212)
XLA Ops:
  1.3 62.0 %shard_map.104 = f32[8,384]{1,0:T(8,128)} custom-call(s32[1]{0:T(128)S(6)} %copy.11.counts_in, s32[2]{0:T(128)} %contact_in.1, f32[4,384]{1,0:T(4,128)} %onsite_in.1, f32[4,384]{1,0:T(4,128)} %hopping_in.1, f32[4,384]{1,0:T(4,128)} %potential_in.1, bf16[4,384,384]{2,1,0:T(8,128)(2,1)} %base_ref.1, bf16[4,384,384]{2,1,0:T(8,128)(2,1)} %wave_ref.1, ...), custom_call_target="tpu_custom_call" | custom-call | tf_op jit(solution)/shard_map/pallas_call | solution.py:511
  63.3 1.4 %fusion = (f32[4,384]{1,0:T(4,128)}, f32[4,384]{1,0:T(4,128)}) fusion(f32[8,384]{1,0:T(8,128)} %shard_map.104), kind=kLoop, calls=%fused_computation | loop fusion | bytes 24576 | tf_op jit(solution)/shard_map/slice | solution.py:554

commit v7 on v6

--- a/solution.py
+++ b/solution.py
@@ -262,17 +262,18 @@
                     l_ref[item, 2 * LANES * i:2 * LANES * i + LANES, sl] = piece[:, :LANES]
                     l_ref[item, 2 * LANES * i + LANES:2 * LANES * (i + 1), sl] = piece[:, LANES:]
 
-        def green(item, s):
+        def green(item, s, last=False):
             br, bi = inverse_diag(item, s)
             brc = jnp.transpose(jnp.broadcast_to(br, (LANES, n)))
             bic = jnp.transpose(jnp.broadcast_to(bi, (LANES, n)))
             for j in range(blocks):
                 lo = LANES * j
                 sl = slice(lo, lo + LANES)
+                end = j + 1 if last else blocks
                 energy_part = lax.dot_general(
-                    c_ref[item, lo:, :], l_ref[item, 2 * lo:2 * lo + 2 * LANES, :], NT, preferred_element_type=f32
+                    c_ref[item, lo:LANES * end, :], l_ref[item, 2 * lo:2 * lo + 2 * LANES, :], NT, preferred_element_type=f32
                 )
-                for i in range(j, blocks):
+                for i in range(j, end):
                     piece = energy_part[LANES * i - lo:LANES * (i + 1) - lo]
                     se_r, se_i = piece[:, :LANES], piece[:, LANES:]
                     cr, ci = brc[LANES * i:LANES * (i + 1)], bic[LANES * i:LANES * (i + 1)]
@@ -287,6 +288,8 @@
                         add_density(
                             s, j, -par_ref[item, 2, 0:1, :] * jnp.sum(jnp.where(eye, gi, 0.0), axis=0, keepdims=True)
                         )
+                    if last:
+                        continue
                     gr, gi = gr.astype(bf16), gi.astype(bf16)
                     si = slice(LANES * i, LANES * (i + 1))
                     g_ref[item, si, 2 * lo:2 * lo + LANES] = gr
@@ -295,7 +298,7 @@
                         g_ref[item, sl, 2 * LANES * i:2 * LANES * i + LANES] = jnp.transpose(gr)
                         g_ref[item, sl, 2 * LANES * i + LANES:2 * LANES * (i + 1)] = jnp.transpose(gi)
 
-        def slab(items, s, between=None):
+        def slab(items, s, between=None, last=False):
             for item in items:
                 couple(item, s)
             for item in items:
@@ -303,7 +306,7 @@
             if between is not None:
                 between()
             for item in items:
-                green(item, s)
+                green(item, s, last)
 
         def own_piece(k):
             return w_ref.at[2 * k + c, rows(part * piece_at, part)]
@@ -386,8 +389,7 @@
         lax.fori_loop(1, slabs, alone(0), 0)
 
         pl.semaphore_wait(barrier, PLANE - 1 + NZ * CORES - 1)
-        mine = jnp.zeros((SUB, LANES), jnp.int32) + counts_ref[0]
-        count_mine[0] = mine.astype(f32)
+        count_mine[0] = counts_ref[...]
 
         def send_count(d):
             return remote(
@@ -457,12 +459,12 @@
             pl.semaphore_signal(plane_ready, 1, device_id=in_plane(d), device_id_type=MESH)
         stage_plane(own_pairs + 2)
 
-        def both(k, carry):
+        def both(k, carry, last=False):
             stage_here(k)
             stage_plane(k + 3)
             slab((0, 1), CORES * k, lambda: stage_chip(k + 1))
             stage_row(k + 5)
-            slab((0, 1), CORES * k + 1)
+            slab((0, 1), CORES * k + 1, last=last)
             @pl.when(k == own_pairs)
             def _():
                 pl.semaphore_wait(plane_ready, PLANE - 1)
@@ -479,7 +481,8 @@
 
             return carry
 
-        lax.fori_loop(own_pairs, pairs, both, 0)
+        lax.fori_loop(own_pairs, pairs - 1, both, 0)
+        both(pairs - 1, 0, True)
         finish()
 
         for d in range(1, PLANE):
@@ -520,7 +523,7 @@
             pltpu.VMEM((3, slabs, n), f32),
             pltpu.VMEM((slabs, n), f32),
             pltpu.VMEM((n, n), f32),
-            pltpu.SMEM((1,), jnp.int32),
+            pltpu.VMEM(tile, f32),
             pltpu.SMEM((2,), jnp.int32),
             pltpu.VMEM((PLANE, *tile), f32),
             pltpu.VMEM((2, *tile), f32),
@@ -550,7 +553,7 @@
             pltpu.SemaphoreType.REGULAR,
         ],
         compiler_params=pltpu.CompilerParams(collective_id=0, has_side_effects=True, vmem_limit_bytes=62 * 2**20),
-    )(counts, contact_slabs, onsite, hopping, potential_in, couple_base, couple_wave, doping, poisson_inverse)
+    )(jnp.broadcast_to(counts.astype(f32).reshape(1, 1), tile), contact_slabs, onsite, hopping, potential_in, couple_base, couple_wave, doping, poisson_inverse)
     return out[:slabs], out[slabs:]
 
 

time: 65 us -> 64.6 us (level)
  Pallas kernels: 62 us -> 61.2 us
    pallas_call x1, Pallas kernels: 62 us -> 61.2 us  [body(): pl.pallas_call(kernel, out_shape=jax.ShapeDtypeStruct((2 * slabs, n), f32...]
where the time goes in v7:
time: 64.6 us; the launch traced here: 64.4 us
  Pallas kernels  61.2 us (95%)
  local copies, waits for them, and re-layouts  1.98 us (3%)
  between operations  1.28 us (2%)
    pallas_call x1, Pallas kernels, body(): pl.pallas_call(kernel, out_shape=jax.ShapeDtypeStruct((2 * slabs, n), f32...  61.2 us
    slice x1, local copies, waits for them, and re-layouts, body(): return (out[:slabs], out[slabs:])  1.38 us

profile of v7, /device:TPU:384, one launch (start us, length us, event | category | flops | bytes accessed | tf_op | source)
XLA Modules:
  0.0 64.4 jit_solution(6637801517988801864)
XLA Ops:
  1.3 0.6 broadcast_in_dim.8.counts_in
  1.9 61.2 %shard_map.104 = f32[8,384]{1,0:T(8,128)} custom-call(f32[8,128]{1,0:T(8,128)} %broadcast_in_dim.8.counts_in, s32[2]{0:T(128)} %contact_in.1, f32[4,384]{1,0:T(4,128)} %onsite_in.1, f32[4,384]{1,0:T(4,128)} %hopping_in.1, f32[4,384]{1,0:T(4,128)} %potential_in.1, bf16[4,384,384]{2,1,0:T(8,128)(2,1)} %base_ref.1, bf16[4,384,384]{2,1,0:T(8,128)(2,1)} %wave_ref.1, ...), custom_call_target="tpu_custom_call" | custom-call | tf_op jit(solution)/shard_map/pallas_call | solution.py:514
  63.0 1.4 %fusion = (f32[4,384]{1,0:T(4,128)}, f32[4,384]{1,0:T(4,128)}) fusion(f32[8,384]{1,0:T(8,128)} %shard_map.104), kind=kLoop, calls=%fused_computation | loop fusion | bytes 24576 | tf_op jit(solution)/shard_map/slice | solution.py:557
